TPU v7x, 512 devices: a whole 4x8x8 slice. The times are simulated.
512 devices in a mesh: blk: 16 (over x_hi, y), grp: 32 (over x_lo, z, core).
Axes of the slice: x: 4 (x_hi: 2, x_lo: 2; x = x_hi * 2 + x_lo), y: 8, z: 8, core: 2. Of those that a mesh axis runs over, the one named last changes fastest.
Arguments:
- blocks: bfloat16 [16, 32, 16, 6, 128, 128], P('blk', 'grp'), may hold values from -0.109375 to 0.109375
- block_row: int32 [16, 32, 16, 6], P('blk', 'grp'), may hold values from 0 to 3
- block_col: int32 [16, 32, 16, 6], P('blk', 'grp'), may hold values from 0 to 3
- probes: bfloat16 [262144, 256], P(('blk', 'grp')), may hold values from -6 to 6
- adjoint_probes: bfloat16 [262144, 256], P(('blk', 'grp')), may hold values from -6 to 6
- row_owner: int32 [262144, 1], P(('blk', 'grp')), may hold values from 0 to 31; in each aligned block of 512 rows (0 to 511, 512 to 1023, ...) at most 32 rows name the same one
Outputs:
- row_samples: bfloat16 [262144, 256], P(('blk', 'grp'))
- column_samples: bfloat16 [262144, 256], P(('blk', 'grp'))
- row_gram: float32 [16, 32, 256, 256], P('blk', 'grp')
- column_gram: float32 [16, 32, 256, 256], P('blk', 'grp')
Inputs may be any that keep to these rules, and one draw needn't show every extreme that they name: `row_owner`: in each aligned block of 512 rows (the rows of one device) no owner is named by more than 32 rows; one owner is named by exactly 32 rows in some blocks.
All inputs are finite; a program needn't handle non-finite values.
Results may differ from a plain program's by a relative error of at most 0.018.
Values may be sent and summed in bfloat16 or wider, within the bound.
No kernel may reach another device: no remote copies, remote signals or barrier semaphores. Data moves between devices by JAX's collectives and lax.ppermute only.
A program may use at most 128 MiB of HBM per device.

v0:
```python
import jax
import jax.numpy as jnp
from jax import lax
from jax.sharding import PartitionSpec as P


def pack_rows(samples, owner, owners, capacity):
    member = (owner == jnp.arange(owners, dtype=jnp.int32)[None, :]).astype(jnp.int32)
    before = jnp.cumsum(member, axis=0) - member
    rank = jnp.sum(before * member, axis=1)
    slot = owner[:, 0] * capacity + rank
    return jnp.zeros((owners * capacity, samples.shape[1]), samples.dtype).at[slot].set(samples)


def owner_gram(received, count):
    gram = lax.dot_general(
        received, received, (((0,), (0,)), ((), ())), preferred_element_type=jnp.float32
    )
    return (gram / count).reshape(1, 1, gram.shape[0], gram.shape[1])


def body(blocks, block_row, block_col, probes, adjoint_probes, row_owner):
    groups = blocks.shape[2]
    per_group = blocks.shape[3]
    side = blocks.shape[4]
    local_blocks = blocks.reshape(groups, per_group, side, side).astype(jnp.float32)
    rows_of = block_row.reshape(groups, per_group)
    cols_of = block_col.reshape(groups, per_group)
    n_rows, width = probes.shape
    per_device = n_rows // side
    owners = lax.axis_size("grp")
    capacity = 2 * n_rows // owners
    group_index = jnp.arange(groups, dtype=jnp.int32)[:, None]
    global_cols = group_index * per_device + cols_of
    assembled = jnp.zeros((per_device, groups * per_device, side, side), jnp.float32)
    assembled = assembled.at[rows_of, global_cols].add(local_blocks)
    dense = jnp.transpose(assembled.astype(jnp.bfloat16), (0, 2, 1, 3)).reshape(
        n_rows, groups * n_rows
    )
    panel_all = lax.all_gather(probes, "blk", axis=0, tiled=True)
    forward = jnp.dot(dense, panel_all, preferred_element_type=jnp.float32)
    row_samples = forward.astype(jnp.bfloat16)
    row_buffer = pack_rows(row_samples, row_owner, owners, capacity)
    column_sum = lax.psum_scatter(
        lax.dot_general(
            dense, adjoint_probes, (((0,), (0,)), ((), ())), preferred_element_type=jnp.float32
        ).astype(jnp.bfloat16),
        "blk",
        scatter_dimension=0,
        tiled=True,
    )
    column_buffer = pack_rows(column_sum, row_owner, owners, capacity)
    row_received, column_received = (
        lax.all_to_all(row_buffer, "grp", split_axis=0, concat_axis=0, tiled=True),
        lax.all_to_all(column_buffer, "grp", split_axis=0, concat_axis=0, tiled=True),
    )
    row_gram = owner_gram(row_received, n_rows)
    column_gram = owner_gram(column_received, n_rows)
    return (row_samples, column_sum, row_gram, column_gram)


def solution(mesh):
    in_specs = (
        P("blk", "grp", None, None, None, None),
        P("blk", "grp", None, None),
        P("blk", "grp", None, None),
        P(("blk", "grp"), None),
        P(("blk", "grp"), None),
        P(("blk", "grp"), None),
    )
    out_specs = (
        P(("blk", "grp"), None),
        P(("blk", "grp"), None),
        P("blk", "grp", None, None),
        P("blk", "grp", None, None),
    )
    return jax.shard_map(body, mesh=mesh, in_specs=in_specs, out_specs=out_specs, check_vma=False)
```

profile of v0, /device:TPU:16, one launch (start us, length us, event | category | flops | bytes accessed | tf_op | source)
XLA Modules:
  0.0 377.8 jit_solution(8434345256429521393)
XLA Ops:
  7.2 0.0 copy-start
  7.2 0.0 all-gather.2.cloned.1.call-start
  7.2 0.7 all-gather.2.cloned.1.call-update
  7.9 0.0 reduce-scatter.2.cloned.1.call-start
  8.0 0.7 or_select_fusion
  8.7 0.1 copy.14
  8.8 0.1 reshape.127
  8.9 5.4 %bitcast_convert_fusion = f32[96,128,128]{2,1,0:T(8,128)} fusion(bf16[1,1,16,6,128,128]{5,4,3,2,1,0:T(8,128)(2,1)} %param.6), kind=kLoop, calls=%fused_computation.10 | loop fusion | flops 1572864 | bytes 9437184 | tf_op jit(solution)/shard_map/convert_element_type | solution.py:26
  14.3 7.8 %broadcast_in_dim.2 = f32[4,64,128,128]{3,2,1,0:T(8,128)} broadcast(f32[]{:T(128)} %constant.8.clone.1), dimensions={} | broadcast | bytes 16777220 | tf_op jit(solution)/shard_map/broadcast_in_dim | solution.py:35
  22.1 20.7 %scatter_fusion = f32[4,64,128,128]{3,2,1,0:T(8,128)} fusion(f32[4,64,128,128]{3,2,1,0:T(8,128)} %broadcast_in_dim.2, s32[96]{0:T(128)S(1)} %reshape.127, f32[96,128,128]{2,1,0:T(8,128)} %bitcast_convert_fusion), kind=kCustom, calls=%fused_computation | custom fusion | flops 1572864 | bytes 18875136 | tf_op jit(solution)/shard_map/scatter-add | solution.py:36
  42.8 9.7 %convert_bitcast_fusion = bf16[4,128,64,128]{3,1,2,0:T(8,128)(2,1)} fusion(f32[4,64,128,128]{3,2,1,0:T(8,128)} %scatter_fusion), kind=kLoop, calls=%fused_computation.7 | loop fusion | flops 4194304 | bytes 25165824 | tf_op jit(solution)/shard_map/transpose | solution.py:37
  52.5 12.1 %copy.15 = bf16[4,128,64,128]{3,2,1,0:T(8,128)(2,1)} copy(bf16[4,128,64,128]{3,1,2,0:T(8,128)(2,1)} %convert_bitcast_fusion) | data formatting | bytes 16777216 | tf_op jit(solution)/shard_map/transpose | solution.py:37
  64.5 0.0 copy-done
  64.5 22.6 %convolution_convert_fusion = bf16[8192,256]{1,0:T(8,128)(2,1)} fusion(bf16[512,256]{1,0:T(8,128)(2,1)S(1)} %copy-done, bf16[64,8,64,128]{3,2,1,0:T(8,128)(2,1)} %bitcast.69), kind=kOutput, calls=%fused_computation.3 | convolution fusion | flops 2149580800 | bytes 12845056 | tf_op jit(solution)/shard_map/dot_general | solution.py:45
  87.1 0.0 reduce-scatter.2.cloned.1.call-update
  87.2 0.0 copy-done.1
  87.2 1.4 reduce-window.6
  88.6 0.2 slice_reduce_fusion
  88.8 0.1 fusion.18
  88.9 31.3 %all-gather.2.cloned.1.call-done = bf16[8192,256]{1,0:T(8,128)(2,1)} async-done(((bf16[512,256]{1,0:T(8,128)(2,1)}), bf16[8192,256]{1,0:T(8,128)(2,1)}) %all-gather.2.cloned.1.call-update) | async-done | bytes 4194320 | tf_op jit(solution)/shard_map/all_gather | solution.py:40
  120.2 9.3 %fusion.5 = bf16[512,256]{1,0:T(8,128)(2,1)S(1)} fusion(bf16[8192,256]{1,0:T(8,128)(2,1)} %all-gather.2.cloned.1.call-done, bf16[64,8,64,128]{3,2,1,0:T(8,128)(2,1)} %bitcast.70), kind=kOutput, calls=%fused_computation.11 | convolution fusion | flops 2147614720 | bytes 12845056 | tf_op jit(solution)/shard_map/dot_general | solution.py:41
  129.5 0.0 copy-start.2
  129.6 3.1 scatter_custom_fusion.1
  132.7 7.8 %all-to-all-start = ((bf16[32,32,256]{2,1,0:T(8,128)(2,1)}), bf16[32,32,256]{2,1,0:T(8,128)(2,1)S(1)}, u32[]{:S(2)}, u32[]{:S(2)}) async-start(bf16[32,32,256]{2,1,0:T(8,128)(2,1)} %bitcast.9), calls=%async_computation.1 | async-start | bytes 1048576 | tf_op jit(solution)/shard_map/all_to_all | solution.py:54
  140.5 199.4 %reduce-scatter.2.cloned.1.call-done = bf16[512,256]{1,0:T(8,128)(2,1)} async-done(((bf16[8192,256]{1,0:T(8,128)(2,1)}), bf16[512,256]{1,0:T(8,128)(2,1)}) %reduce-scatter.2.cloned.1.call-update) | async-done | bytes 262160 | tf_op jit(solution)/shard_map/reduce_scatter | solution.py:44
  339.8 3.5 scatter_custom_fusion.2
  343.4 0.0 all-to-all-done
  343.4 7.8 %all-to-all-start.1 = ((bf16[32,32,256]{2,1,0:T(8,128)(2,1)}), bf16[32,32,256]{2,1,0:T(8,128)(2,1)S(1)}, u32[]{:S(2)}, u32[]{:S(2)}) async-start(bf16[32,32,256]{2,1,0:T(8,128)(2,1)} %bitcast.12), calls=%async_computation.2 | async-start | bytes 1048576 | tf_op jit(solution)/shard_map/all_to_all | solution.py:55
  351.2 1.0 fusion.10
  352.2 17.4 %all-to-all-done.1 = bf16[32,32,256]{2,1,0:T(8,128)(2,1)S(1)} async-done(((bf16[32,32,256]{2,1,0:T(8,128)(2,1)}), bf16[32,32,256]{2,1,0:T(8,128)(2,1)S(1)}, u32[]{:S(2)}, u32[]{:S(2)}) %all-to-all-start.1) | async-done | bytes 524320 | tf_op jit(solution)/shard_map/all_to_all | solution.py:55
  369.6 1.0 fusion.11
  370.7 0.0 copy-done.2
  (6 shorter events, 0.1 us)
Async XLA Ops:
  7.2 57.4 %copy-start = (bf16[512,256]{1,0:T(8,128)(2,1)S(1)}, bf16[512,256]{1,0:T(8,128)(2,1)}, u32[]{:S(2)}) copy-start(bf16[512,256]{1,0:T(8,128)(2,1)} %param.10) | copy-start | bytes 786436
  7.2 113.1 %all-gather.2.cloned.1.call-start = ((), (), s32[]{:S(2)}) async-start(), calls=%async_computation.3 | async-start | bytes 4456448 | tf_op jit(solution)/shard_map/all_gather | solution.py:40
  7.9 331.9 %reduce-scatter.2.cloned.1.call-start = ((), (), s32[]{:S(2)}) async-start(), calls=%async_computation.4 | async-start | bytes 4456448 | tf_op jit(solution)/shard_map/reduce_scatter | solution.py:44
  64.5 22.6 %copy-start.1 = (s32[512,1]{0,1:T(1,128)S(1)}, s32[512,1]{0,1:T(1,128)}, u32[]{:S(2)}) copy-start(s32[512,1]{0,1:T(1,128)} %param.11) | copy-start | bytes 6148
  129.5 241.1 %copy-start.2 = (bf16[512,256]{1,0:T(8,128)(2,1)}, bf16[512,256]{1,0:T(8,128)(2,1)S(1)}, u32[]{:S(2)}) copy-start(bf16[512,256]{1,0:T(8,128)(2,1)S(1)} %fusion.5) | copy-start | bytes 786436
  132.7 210.7 %all-to-all-start = ((bf16[32,32,256]{2,1,0:T(8,128)(2,1)}), bf16[32,32,256]{2,1,0:T(8,128)(2,1)S(1)}, u32[]{:S(2)}, u32[]{:S(2)}) async-start(bf16[32,32,256]{2,1,0:T(8,128)(2,1)} %bitcast.9), calls=%async_computation.1 | async-start | bytes 1048576 | tf_op jit(solution)/shard_map/all_to_all | solution.py:54
  343.4 26.3 %all-to-all-start.1 = ((bf16[32,32,256]{2,1,0:T(8,128)(2,1)}), bf16[32,32,256]{2,1,0:T(8,128)(2,1)S(1)}, u32[]{:S(2)}, u32[]{:S(2)}) async-start(bf16[32,32,256]{2,1,0:T(8,128)(2,1)} %bitcast.12), calls=%async_computation.2 | async-start | bytes 1048576 | tf_op jit(solution)/shard_map/all_to_all | solution.py:55
Sparse Core Ops, SparseCore 0:
  11.2 109.0 all-gather.1
  125.4 214.3 reduce-scatter.1
where the time goes:
time: 381 us; the launch traced here: 378 us
  waiting for transfers between devices  249 us (65%)
  other arithmetic  38 us (10%)
  matrix products  34 us (9%)
  local copies, waits for them, and re-layouts  27 us (7%)
  starting transfers between devices  15.7 us (4%)
  between operations  14.4 us (4%)
    reduce_scatter x1, waiting for transfers between devices, body(): lax.psum_scatter(lax.dot_general(dense, adjoint_probes, (((0,), (0,)), ((...  199 us
    all_gather x1, waiting for transfers between devices, body(): panel_all = lax.all_gather(probes, 'blk', axis=0, tiled=True)  31.3 us
    dot_general x1, matrix products, body(): lax.dot_general(dense, adjoint_probes, (((0,), (0,)), ((), ())), preferre...  22.6 us
    scatter-add x1, other arithmetic, body(): assembled = assembled.at[rows_of, global_cols].add(local_blocks)  20.7 us
    all_to_all x1, waiting for transfers between devices, body(): lax.all_to_all(column_buffer, 'grp', split_axis=0, concat_axis=0, tiled=T...  17.4 us
    transpose x1, local copies, waits for them, and re-layouts, body(): jnp.transpose(assembled.astype(jnp.bfloat16), (0, 2, 1, 3))  12.1 us
    transpose x1, other arithmetic, body(): jnp.transpose(assembled.astype(jnp.bfloat16), (0, 2, 1, 3))  9.67 us
    dot_general x1, matrix products, body(): forward = jnp.dot(dense, panel_all, preferred_element_type=jnp.float32)  9.28 us
  transfers between devices with their start and end apart: 4, of which 3 were waited for; matrix products, arithmetic and copies ran while one was open for 26% of the time, Pallas kernels for 0%

commit v1 on v0

v1 whole, which is shorter than its diff:
```python
import functools

import jax
import jax.numpy as jnp
from jax import lax
from jax.experimental import pallas as pl
from jax.experimental.pallas import tpu as pltpu
from jax.sharding import PartitionSpec as P

F32 = jnp.float32
BF16 = jnp.bfloat16
PARTS = (3, 3, 2)


def params(mib):
    return pltpu.CompilerParams(vmem_limit_bytes=mib * 1024 * 1024)


ANY = pl.BlockSpec(memory_space=pl.ANY)
VMEM = pl.BlockSpec(memory_space=pltpu.VMEM)
SMEM = pl.BlockSpec(memory_space=pltpu.SMEM)
HBM = pl.BlockSpec(memory_space=pltpu.HBM)


def arrange_kernel(first_ref, a_ref, _, *refs):
    outs, sems = refs[:-1], refs[-1]
    copies = []
    for out, size in zip(outs, PARTS):
        for n in range(size):
            t = len(copies)
            copies.append(pltpu.make_async_copy(a_ref.at[first_ref[0] + t], out.at[n], sems.at[t]))
            copies[-1].start()
    for copy in copies:
        copy.wait()


def arrange(first, blocks, before):
    _, k, side, _ = blocks.shape
    return pl.pallas_call(
        arrange_kernel,
        in_specs=[SMEM, VMEM, ANY],
        out_specs=[HBM] * len(PARTS),
        out_shape=[pltpu.HBM((size, k, side, side), blocks.dtype) for size in PARTS],
        scratch_shapes=[pltpu.SemaphoreType.DMA((sum(PARTS),))],
        compiler_params=params(6),
        name="arrange",
    )(first, blocks, before)


def turn_kernel(q_ref, code_ref, qx_ref):
    rows, width = q_ref.shape
    qx_ref[0:width, :] = q_ref[...].T
    qx_ref[width:, :] = jnp.broadcast_to(code_ref[...], (qx_ref.shape[0] - width, rows)).astype(BF16)


def turn(q, codes):
    rows, width = q.shape
    return pl.pallas_call(
        turn_kernel,
        out_shape=jax.ShapeDtypeStruct((width + 16, rows), BF16),
        compiler_params=params(6),
        name="turn",
    )(q, codes)


def slots_kernel(owners, capacity, owner_ref, _, slot_ref):
    owner = owner_ref[...]
    rows = owner.shape[1]
    member = lax.broadcasted_iota(jnp.int32, (owners, rows), 0) == owner
    earlier = lax.broadcasted_iota(jnp.int32, (rows, rows), 0) < lax.broadcasted_iota(jnp.int32, (rows, rows), 1)
    before = jnp.dot(member.astype(BF16), earlier.astype(BF16), preferred_element_type=F32)
    rank = jnp.sum(jnp.where(member, before, 0.0), axis=0, keepdims=True)
    slot_ref[...] = owner * capacity + rank.astype(jnp.int32)


def slots_of(owner, owners, capacity, before):
    return pl.pallas_call(
        functools.partial(slots_kernel, owners, capacity),
        in_specs=[VMEM, ANY],
        out_specs=VMEM,
        out_shape=jax.ShapeDtypeStruct(owner.shape, jnp.int32),
        compiler_params=params(6),
        name="slots",
    )(owner, before)


def strip_kernel(start, first_ref, mine_ref, theirs_ref, q_ref, qp_ref, a_ref, b_ref, *refs):
    c_ref, d_ref = refs[-2:]
    k = a_ref.shape[1]
    side = a_ref.shape[2]
    rows = d_ref.shape[1] // 2
    per = rows // side
    width = c_ref.shape[1]
    d_ref[...] = jnp.zeros(d_ref.shape, d_ref.dtype)
    source = first_ref[0] + start + pl.program_id(0)
    for base, codes, blk in ((0, mine_ref, a_ref), (rows, theirs_ref, b_ref)):
        for n in range(k):
            code = codes[source * k + n]
            at_row = pl.multiple_of(base + (code // per) * side, side)
            at_col = pl.multiple_of((code % per) * side, side)
            place = (0, pl.ds(at_row, side), pl.ds(at_col, side))
            d_ref[place] = (d_ref[place].astype(F32) + blk[0, n].astype(F32)).astype(d_ref.dtype)
    term = jnp.dot(q_ref[0:width, :], d_ref[0, 0:rows, :], preferred_element_type=F32)
    term += jnp.dot(qp_ref[0:width, :], d_ref[0, rows:, :], preferred_element_type=F32)
    c_ref[0] = term.astype(c_ref.dtype)


def strips(start, first, mine, theirs, qx, qx_partner, blocks, received, width, held):
    _, k, side, _ = blocks.shape
    rows = qx.shape[1]
    size, groups = received.shape[0], sum(PARTS)
    whole = pl.BlockSpec(qx.shape, lambda i, *_: (0, 0))
    return pl.pallas_call(
        functools.partial(strip_kernel, start),
        grid_spec=pltpu.PrefetchScalarGridSpec(
            num_scalar_prefetch=3,
            grid=(size,),
            in_specs=[
                whole,
                whole,
                pl.BlockSpec((1, k, side, side), lambda i, first, *_: (first[0] + start + i, 0, 0, 0)),
                pl.BlockSpec((1, k, side, side), lambda i, *_: (i, 0, 0, 0)),
            ]
            + [HBM] * len(held),
            out_specs=[
                pl.BlockSpec((1, width, rows), lambda i, *_: (start + i, 0, 0)),
                pl.BlockSpec((1, 2 * rows, rows), lambda i, *_: (start + i, 0, 0)),
            ],
        ),
        out_shape=[
            pltpu.HBM((groups, width, rows), BF16),
            pltpu.HBM((groups, 2 * rows, rows), BF16),
        ],
        input_output_aliases={7 + n: n for n in range(len(held))},
        compiler_params=params(10),
        name="strips",
    )(first, mine, theirs, qx, qx_partner, blocks, received, *held)


def forward_kernel(d_ref, p_ref, own_ref, send_ref, total_ref):
    step = pl.program_id(0)
    rows = own_ref.shape[0]
    term = sum(jnp.dot(d_ref[n], p_ref[n], preferred_element_type=F32) for n in range(d_ref.shape[0]))

    @pl.when(step == 0)
    def _():
        total_ref[...] = term

    @pl.when(step > 0)
    def _():
        total_ref[...] += term

    @pl.when(step == pl.num_programs(0) - 1)
    def _():
        own_ref[...] = total_ref[0:rows, :]
        send_ref[...] = total_ref[rows:, :].astype(send_ref.dtype)


def forward(dense, panels):
    groups, rows, width = panels.shape
    whole = pl.BlockSpec((rows, width), lambda i: (0, 0))
    return pl.pallas_call(
        forward_kernel,
        grid=(groups // 2,),
        in_specs=[
            pl.BlockSpec((2, 2 * rows, rows), lambda i: (i, 0, 0)),
            pl.BlockSpec((2, rows, width), lambda i: (i, 0, 0)),
        ],
        out_specs=[whole, whole],
        scratch_shapes=[pltpu.VMEM((2 * rows, width), F32)],
        out_shape=[jax.ShapeDtypeStruct((rows, width), F32), jax.ShapeDtypeStruct((rows, width), BF16)],
        compiler_params=params(20),
        name="forward",
    )(pltpu.with_memory_space_constraint(dense, pltpu.HBM), panels)


def one_hot(slot, slots):
    return (lax.broadcasted_iota(jnp.int32, (slots, slot.shape[1]), 0) == slot).astype(BF16)


def pack_rows_kernel(own_ref, got_ref, slot_ref, samples_ref, packed_ref):
    samples = (own_ref[...] + got_ref[...].astype(F32)).astype(BF16)
    samples_ref[...] = samples
    packed_ref[...] = jnp.dot(
        one_hot(slot_ref[...], packed_ref.shape[0]), samples, preferred_element_type=F32
    ).astype(BF16)


def pack_rows(own, got, slot, slots):
    rows, width = own.shape
    return pl.pallas_call(
        pack_rows_kernel,
        out_shape=[jax.ShapeDtypeStruct((rows, width), BF16), jax.ShapeDtypeStruct((slots, width), BF16)],
        compiler_params=params(8),
        name="pack_rows",
    )(own, got, slot)


def pack_columns_kernel(samples_ref, slot_ref, _, packed_ref):
    packed_ref[...] = lax.dot_general(
        one_hot(slot_ref[...], packed_ref.shape[0]),
        samples_ref[...],
        (((1,), (1,)), ((), ())),
        preferred_element_type=F32,
    ).astype(BF16)


def pack_columns(samples, slot, slots, before):
    return pl.pallas_call(
        pack_columns_kernel,
        in_specs=[VMEM, VMEM, ANY],
        out_specs=VMEM,
        out_shape=jax.ShapeDtypeStruct((slots, samples.shape[0]), BF16),
        compiler_params=params(8),
        name="pack_columns",
    )(samples, slot, before)


def owner_gram(received, count):
    gram = lax.dot_general(received, received, (((0,), (0,)), ((), ())), preferred_element_type=F32)
    return (gram / count)[None, None]


def body(blocks, block_row, block_col, probes, adjoint_probes, row_owner):
    groups, per_group, side = blocks.shape[2], blocks.shape[3], blocks.shape[4]
    blocks = blocks.reshape(groups, per_group, side, side)
    n_rows, width = probes.shape
    owners = lax.axis_size("grp")
    capacity = 2 * n_rows // owners
    slots = owners * capacity
    ring = groups // 2
    half = lax.axis_index("blk") // ring
    kept, crossing = (half * ring).reshape(1), ((1 - half) * ring).reshape(1)
    across = [(b, (b + ring) % groups) for b in range(groups)]
    halves = [list(range(ring)), list(range(ring, groups))]

    codes = (block_row * (n_rows // side) + block_col).reshape(groups * per_group)
    code_row = jnp.pad(codes.astype(F32), (0, n_rows - codes.shape[0])).reshape(1, n_rows)
    qx = turn(adjoint_probes, code_row)
    leaving = arrange(crossing, blocks, qx)
    panels = lax.all_gather(probes, "blk", axis=0, tiled=True, axis_index_groups=halves).reshape(ring, n_rows, width)
    qx_partner = lax.ppermute(qx, "blk", across)
    received = [lax.ppermute(part, "blk", across) for part in leaving]
    partner_codes = qx_partner[width, 0 : codes.shape[0]].astype(jnp.int32)
    slot = slots_of(row_owner.reshape(1, n_rows), owners, capacity, partner_codes)

    held = ()
    for j in range(len(PARTS)):
        held = strips(
            sum(PARTS[:j]), kept, codes, partner_codes, qx, qx_partner, blocks, received[j], width, held
        )
    terms, dense = held
    columns = lax.psum_scatter(terms, "blk", scatter_dimension=0, tiled=False, axis_index_groups=halves)
    own, partial = forward(dense, panels)
    got = lax.ppermute(partial, "blk", across)
    row_samples, row_packed = pack_rows(own, got, slot, slots)
    row_received = lax.all_to_all(row_packed.reshape(owners, capacity, width), "grp", 0, 0, tiled=True)
    column_packed = pack_columns(columns, slot, slots, row_received)
    column_received = lax.all_to_all(column_packed.reshape(owners, capacity, width), "grp", 0, 0, tiled=True)
    row_gram = owner_gram(row_received.reshape(slots, width), n_rows)
    column_gram = owner_gram(column_received.reshape(slots, width), n_rows)
    return (row_samples, columns.T, row_gram, column_gram)


def solution(mesh):
    in_specs = (
        P("blk", "grp", None, None, None, None),
        P("blk", "grp", None, None),
        P("blk", "grp", None, None),
        P(("blk", "grp"), None),
        P(("blk", "grp"), None),
        P(("blk", "grp"), None),
    )
    out_specs = (
        P(("blk", "grp"), None),
        P(("blk", "grp"), None),
        P("blk", "grp", None, None),
        P("blk", "grp", None, None),
    )
    return jax.shard_map(body, mesh=mesh, in_specs=in_specs, out_specs=out_specs, check_vma=False)
```

time: 381 us -> 153 us (0.40)
  the two profiles are of different devices: /device:TPU:16 before, /device:TPU:24 now
where the time goes in v1:
time: 153 us; the launch traced here: 152 us
  waiting for transfers between devices  63.8 us (42%)
  starting transfers between devices  40.1 us (26%)
  Pallas kernels  23 us (15%)
  between operations  14.2 us (9%)
  local copies, waits for them, and re-layouts  7.34 us (5%)
  matrix products  2.09 us (1%)
    ppermute x1, waiting for transfers between devices, body(): qx_partner = lax.ppermute(qx, 'blk', across)  23.8 us
    reduce_scatter x1, waiting for transfers between devices, body(): lax.psum_scatter(terms, 'blk', scatter_dimension=0, tiled=False, axis_ind...  19 us
    all_to_all x1, waiting for transfers between devices, body(): lax.all_to_all(column_packed.reshape(owners, capacity, width), 'grp', 0,...  15.6 us
    pallas_call x3, Pallas kernels, strips(): pl.pallas_call(functools.partial(strip_kernel, start), grid_spec=pltpu.Pr...  13.1 us
    all_to_all x1, starting transfers between devices, body(): lax.all_to_all(row_packed.reshape(owners, capacity, width), 'grp', 0, 0,...  11.6 us
    ppermute x3, starting transfers between devices, body(): received = [lax.ppermute(part, 'blk', across) for part in leaving]  9.9 us
    all_to_all x1, starting transfers between devices, body(): lax.all_to_all(column_packed.reshape(owners, capacity, width), 'grp', 0,...  8.65 us
    unnamed x13, local copies, waits for them, and re-layouts  7.16 us
  transfers between devices with their start and end apart: 9, of which 4 were waited for; matrix products, arithmetic and copies ran while one was open for 3% of the time, Pallas kernels for 14%

profile of v1, /device:TPU:24, one launch (start us, length us, event | category | flops | bytes accessed | tf_op | source)
XLA Modules:
  0.0 152.0 jit_solution(3411576641245943320)
XLA Ops:
  7.2 0.7 all-gather.2.cloned.1.call-update
  8.0 0.7 multiply_add_fusion
  8.7 0.1 copy.16
  8.7 0.1 reshape.40.mine_ref
  8.9 0.9 copy-done.4
  9.8 0.1 turn.1._.q_ref
  10.0 1.9 %copy-done = bf16[1,1,16,6,128,128]{5,4,3,2,1,0:T(8,128)(2,1)S(1)} copy-done((bf16[1,1,16,6,128,128]{5,4,3,2,1,0:T(8,128)(2,1)S(1)}, bf16[1,1,16,6,128,128]{5,4,3,2,1,0:T(8,128)(2,1)}, u32[]{:S(2)}) %copy-start) | copy-done | bytes 3145752
  11.9 1.3 arrange.1
  13.1 5.1 %collective-permute-start.3 = (bf16[3,6,128,128]{3,2,1,0:T(8,128)(2,1)}, bf16[3,6,128,128]{3,2,1,0:T(8,128)(2,1)}, u32[]{:S(2)}, u32[]{:S(2)}) collective-permute-start(bf16[3,6,128,128]{3,2,1,0:T(8,128)(2,1)} %get-tuple-element.19), channel_id=1, source_target_pairs={{0,256},{32,288},{64,320},{96,352},{128,384},{160,416},{192,448},{... | collective-permute-start | bytes 1769480 | tf_op jit(solution)/shard_map/ppermute | solution.py:243
  18.2 2.4 %collective-permute-start.2 = (bf16[3,6,128,128]{3,2,1,0:T(8,128)(2,1)}, bf16[3,6,128,128]{3,2,1,0:T(8,128)(2,1)}, u32[]{:S(2)}, u32[]{:S(2)}) collective-permute-start(bf16[3,6,128,128]{3,2,1,0:T(8,128)(2,1)} %get-tuple-element.18), channel_id=1, source_target_pairs={{0,256},{32,288},{64,320},{96,352},{128,384},{160,416},{192,448},{... | collective-permute-start | bytes 1769480 | tf_op jit(solution)/shard_map/ppermute | solution.py:243
  20.6 4.9 %collective-permute-start = (bf16[272,512]{1,0:T(8,128)(2,1)S(1)}, bf16[272,512]{1,0:T(8,128)(2,1)}, u32[]{:S(2)}, u32[]{:S(2)}) collective-permute-start(bf16[272,512]{1,0:T(8,128)(2,1)S(1)} %turn.1._.q_ref), channel_id=1, source_target_pairs={{0,256},{32,288},{64,320},{96,352},{128,384},{160,416},{192,448},{... | collective-permute-start | bytes 835592 | tf_op jit(solution)/shard_map/ppermute | solution.py:242
  25.6 2.4 %collective-permute-start.1 = (bf16[2,6,128,128]{3,2,1,0:T(8,128)(2,1)}, bf16[2,6,128,128]{3,2,1,0:T(8,128)(2,1)}, u32[]{:S(2)}, u32[]{:S(2)}) collective-permute-start(bf16[2,6,128,128]{3,2,1,0:T(8,128)(2,1)} %get-tuple-element.17), channel_id=1, source_target_pairs={{0,256},{32,288},{64,320},{96,352},{128,384},{160,416},{192,448},{... | collective-permute-start | bytes 1179656 | tf_op jit(solution)/shard_map/ppermute | solution.py:243
  28.0 23.8 %collective-permute-done.qp_ref = bf16[272,512]{1,0:T(8,128)(2,1)} collective-permute-done((bf16[272,512]{1,0:T(8,128)(2,1)S(1)}, bf16[272,512]{1,0:T(8,128)(2,1)}, u32[]{:S(2)}, u32[]{:S(2)}) %collective-permute-start) | collective-permute-done | bytes 278560 | tf_op jit(solution)/shard_map/ppermute | solution.py:242
  51.8 0.7 fusion.4.theirs_ref._
  52.5 4.7 %strips.3 = (bf16[8,256,512]{2,1,0:T(8,128)(2,1)}, bf16[8,1024,512]{2,1,0:T(8,128)(2,1)}) custom-call(s32[1]{0:T(128)} %bitcast.first_ref, s32[96]{0:T(128)S(1)} %reshape.40.mine_ref, s32[96]{0:T(128)S(1)} %fusion.4.theirs_ref._, bf16[272,512]{1,0:T(8,128)(2,1)S(1)} %turn.1._.q_ref, bf16[272,512]{1,0:T(8,128)(2,1)} %collective-permute-done.qp_ref, ...), custom_call_target="tpu_custom_call" | custom-call | tf_op jit(solution)/shard_map/strips/pallas_call | solution.py:113
  57.2 4.7 %strips.4 = (bf16[8,256,512]{2,1,0:T(8,128)(2,1)}, bf16[8,1024,512]{2,1,0:T(8,128)(2,1)}) custom-call(s32[1]{0:T(128)} %bitcast.first_ref, s32[96]{0:T(128)S(1)} %reshape.40.mine_ref, s32[96]{0:T(128)S(1)} %fusion.4.theirs_ref._, bf16[272,512]{1,0:T(8,128)(2,1)S(1)} %turn.1._.q_ref, ...), custom_call_target="tpu_custom_call", output_to_operand_aliasing={{0}: (7, {}), {1}: (8, {})} | custom-call | tf_op jit(solution)/shard_map/strips/pallas_call | solution.py:113
  61.9 3.7 %strips.5 = (bf16[8,256,512]{2,1,0:T(8,128)(2,1)}, bf16[8,1024,512]{2,1,0:T(8,128)(2,1)}) custom-call(s32[1]{0:T(128)} %bitcast.first_ref, s32[96]{0:T(128)S(1)} %reshape.40.mine_ref, s32[96]{0:T(128)S(1)} %fusion.4.theirs_ref._, bf16[272,512]{1,0:T(8,128)(2,1)S(1)} %turn.1._.q_ref, ...), custom_call_target="tpu_custom_call", output_to_operand_aliasing={{0}: (7, {}), {1}: (8, {})} | custom-call | tf_op jit(solution)/shard_map/strips/pallas_call | solution.py:113
  65.6 1.6 %copy-done.2 = bf16[4096,256]{1,0:T(8,128)(2,1)S(1)} copy-done((bf16[4096,256]{1,0:T(8,128)(2,1)S(1)}, bf16[4096,256]{1,0:T(8,128)(2,1)}, u32[]{:S(2)}) %copy-start.2) | copy-done | bytes 2097176
  67.2 5.8 %forward.1 = (f32[512,256]{1,0:T(8,128)S(1)}, bf16[512,256]{1,0:T(8,128)(2,1)S(1)}) custom-call(bf16[8,1024,512]{2,1,0:T(8,128)(2,1)} %get-tuple-element.24.d_ref, bf16[8,512,256]{2,1,0:T(8,128)(2,1)S(1)} %bitcast.42), custom_call_target="tpu_custom_call" | custom-call | tf_op jit(solution)/shard_map/forward/pallas_call | solution.py:162
  73.1 4.9 %collective-permute-start.4 = (bf16[512,256]{1,0:T(8,128)(2,1)S(1)}, bf16[512,256]{1,0:T(8,128)(2,1)S(1)}, u32[]{:S(2)}, u32[]{:S(2)}) collective-permute-start(bf16[512,256]{1,0:T(8,128)(2,1)S(1)} %get-tuple-element.26), channel_id=1, source_target_pairs={{0,256},{32,288},{64,320},{96,352},{128,384},{160,416},{192,448},{... | collective-permute-start | bytes 786440 | tf_op jit(solution)/shard_map/ppermute | solution.py:255
  78.0 0.2 slots.1.slot_ref
  78.2 4.6 %collective-permute-done.4.got_ref = bf16[512,256]{1,0:T(8,128)(2,1)S(1)} collective-permute-done((bf16[512,256]{1,0:T(8,128)(2,1)S(1)}, bf16[512,256]{1,0:T(8,128)(2,1)S(1)}, u32[]{:S(2)}, u32[]{:S(2)}) %collective-permute-start.4) | collective-permute-done | bytes 262176 | tf_op jit(solution)/shard_map/ppermute | solution.py:255
  82.8 1.3 pack_rows.1
  84.1 11.6 %all-to-all-start = ((bf16[32,32,256]{2,1,0:T(8,128)(2,1)}), bf16[32,32,256]{2,1,0:T(8,128)(2,1)S(1)}, u32[]{:S(2)}, u32[]{:S(2)}) async-start(bf16[32,32,256]{2,1,0:T(8,128)(2,1)} %bitcast.10), calls=%async_computation.1 | async-start | bytes 1048576 | tf_op jit(solution)/shard_map/all_to_all | solution.py:257
  95.7 19.0 %reduce-scatter.2.cloned.1.call-done = bf16[1,256,512]{2,1,0:T(8,128)(2,1)} async-done(((bf16[8,256,512]{2,1,0:T(8,128)(2,1)}), bf16[1,256,512]{2,1,0:T(8,128)(2,1)}) %reduce-scatter.2.cloned.1.call-update) | async-done | bytes 262160 | tf_op jit(solution)/shard_map/reduce_scatter | solution.py:253
  114.8 0.9 copy-done.3
  115.7 1.3 pack_columns.1
  117.0 8.7 %all-to-all-start.1 = ((bf16[32,32,256]{2,1,0:T(8,128)(2,1)}), bf16[32,32,256]{2,1,0:T(8,128)(2,1)S(1)}, u32[]{:S(2)}, u32[]{:S(2)}) async-start(bf16[32,32,256]{2,1,0:T(8,128)(2,1)} %bitcast.13), calls=%async_computation.2 | async-start | bytes 1048576 | tf_op jit(solution)/shard_map/all_to_all | solution.py:259
  125.6 1.8 %copy.17 = bf16[512,256]{1,0:T(8,128)(2,1)} copy(bf16[512,256]{0,1:T(8,128)(2,1)} %bitcast.43) | data formatting | bytes 524288
  127.4 1.0 fusion.2
  128.5 15.6 %all-to-all-done.1 = bf16[32,32,256]{2,1,0:T(8,128)(2,1)S(1)} async-done(((bf16[32,32,256]{2,1,0:T(8,128)(2,1)}), bf16[32,32,256]{2,1,0:T(8,128)(2,1)S(1)}, u32[]{:S(2)}, u32[]{:S(2)}) %all-to-all-start.1) | async-done | bytes 524320 | tf_op jit(solution)/shard_map/all_to_all | solution.py:259
  144.1 1.0 fusion.3
  (18 shorter events, 0.2 us)
Async XLA Ops:
  7.2 58.4 %all-gather.2.cloned.1.call-start = ((), (), s32[]{:S(2)}) async-start(), calls=%async_computation.3 | async-start | bytes 2359296 | tf_op jit(solution)/shard_map/all_gather | solution.py:241
  7.9 106.9 %reduce-scatter.2.cloned.1.call-start = ((), (), s32[]{:S(2)}) async-start(), calls=%async_computation.4 | async-start | bytes 2359296 | tf_op jit(solution)/shard_map/reduce_scatter | solution.py:253
  8.9 1.0 copy-start.4
  10.0 1.9 %copy-start = (bf16[1,1,16,6,128,128]{5,4,3,2,1,0:T(8,128)(2,1)S(1)}, bf16[1,1,16,6,128,128]{5,4,3,2,1,0:T(8,128)(2,1)}, u32[]{:S(2)}) copy-start(bf16[1,1,16,6,128,128]{5,4,3,2,1,0:T(8,128)(2,1)} %param.6) | copy-start | bytes 9437188
  11.9 40.6 %copy-start.1 = (bf16[1,1,16,6,128,128]{5,4,3,2,1,0:T(8,128)(2,1)S(1)}, bf16[1,1,16,6,128,128]{5,4,3,2,1,0:T(8,128)(2,1)}, u32[]{:S(2)}) copy-start(bf16[1,1,16,6,128,128]{5,4,3,2,1,0:T(8,128)(2,1)} %param.6) | copy-start | bytes 9437188
  13.1 39.4 %collective-permute-start.3 = (bf16[3,6,128,128]{3,2,1,0:T(8,128)(2,1)}, bf16[3,6,128,128]{3,2,1,0:T(8,128)(2,1)}, u32[]{:S(2)}, u32[]{:S(2)}) collective-permute-start(bf16[3,6,128,128]{3,2,1,0:T(8,128)(2,1)} %get-tuple-element.19), channel_id=1, source_target_pairs={{0,256},{32,288},{64,320},{96,352},{128,384},{160,416},{192,448},{... | collective-permute-start | bytes 1769480 | tf_op jit(solution)/shard_map/ppermute | solution.py:243
  18.2 39.0 %collective-permute-start.2 = (bf16[3,6,128,128]{3,2,1,0:T(8,128)(2,1)}, bf16[3,6,128,128]{3,2,1,0:T(8,128)(2,1)}, u32[]{:S(2)}, u32[]{:S(2)}) collective-permute-start(bf16[3,6,128,128]{3,2,1,0:T(8,128)(2,1)} %get-tuple-element.18), channel_id=1, source_target_pairs={{0,256},{32,288},{64,320},{96,352},{128,384},{160,416},{192,448},{... | collective-permute-start | bytes 1769480 | tf_op jit(solution)/shard_map/ppermute | solution.py:243
  20.6 31.2 %collective-permute-start = (bf16[272,512]{1,0:T(8,128)(2,1)S(1)}, bf16[272,512]{1,0:T(8,128)(2,1)}, u32[]{:S(2)}, u32[]{:S(2)}) collective-permute-start(bf16[272,512]{1,0:T(8,128)(2,1)S(1)} %turn.1._.q_ref), channel_id=1, source_target_pairs={{0,256},{32,288},{64,320},{96,352},{128,384},{160,416},{192,448},{... | collective-permute-start | bytes 835592 | tf_op jit(solution)/shard_map/ppermute | solution.py:242
  25.6 36.3 %collective-permute-start.1 = (bf16[2,6,128,128]{3,2,1,0:T(8,128)(2,1)}, bf16[2,6,128,128]{3,2,1,0:T(8,128)(2,1)}, u32[]{:S(2)}, u32[]{:S(2)}) collective-permute-start(bf16[2,6,128,128]{3,2,1,0:T(8,128)(2,1)} %get-tuple-element.17), channel_id=1, source_target_pairs={{0,256},{32,288},{64,320},{96,352},{128,384},{160,416},{192,448},{... | collective-permute-start | bytes 1179656 | tf_op jit(solution)/shard_map/ppermute | solution.py:243
  65.6 1.6 %copy-start.2 = (bf16[4096,256]{1,0:T(8,128)(2,1)S(1)}, bf16[4096,256]{1,0:T(8,128)(2,1)}, u32[]{:S(2)}) copy-start(bf16[4096,256]{1,0:T(8,128)(2,1)} %all-gather.2.cloned.1.call-done) | copy-start | bytes 6291460
  67.2 10.8 %copy-start.5 = (s32[512,1]{0,1:T(1,128)S(1)}, s32[512,1]{0,1:T(1,128)}, u32[]{:S(2)}) copy-start(s32[512,1]{0,1:T(1,128)} %param.11) | copy-start | bytes 6148
  73.1 9.8 %collective-permute-start.4 = (bf16[512,256]{1,0:T(8,128)(2,1)S(1)}, bf16[512,256]{1,0:T(8,128)(2,1)S(1)}, u32[]{:S(2)}, u32[]{:S(2)}) collective-permute-start(bf16[512,256]{1,0:T(8,128)(2,1)S(1)} %get-tuple-element.26), channel_id=1, source_target_pairs={{0,256},{32,288},{64,320},{96,352},{128,384},{160,416},{192,448},{... | collective-permute-start | bytes 786440 | tf_op jit(solution)/shard_map/ppermute | solution.py:255
  84.1 30.7 %all-to-all-start = ((bf16[32,32,256]{2,1,0:T(8,128)(2,1)}), bf16[32,32,256]{2,1,0:T(8,128)(2,1)S(1)}, u32[]{:S(2)}, u32[]{:S(2)}) async-start(bf16[32,32,256]{2,1,0:T(8,128)(2,1)} %bitcast.10), calls=%async_computation.1 | async-start | bytes 1048576 | tf_op jit(solution)/shard_map/all_to_all | solution.py:257
  114.8 1.0 copy-start.3
  117.0 27.1 %all-to-all-start.1 = ((bf16[32,32,256]{2,1,0:T(8,128)(2,1)}), bf16[32,32,256]{2,1,0:T(8,128)(2,1)S(1)}, u32[]{:S(2)}, u32[]{:S(2)}) async-start(bf16[32,32,256]{2,1,0:T(8,128)(2,1)} %bitcast.13), calls=%async_computation.2 | async-start | bytes 1048576 | tf_op jit(solution)/shard_map/all_to_all | solution.py:259
Sparse Core Ops, SparseCore 0:
  10.1 47.3 all-gather.1
  65.7 49.0 reduce-scatter.1

commit v2 on v1

--- a/solution.py
+++ b/solution.py
@@ -22,45 +22,52 @@
 HBM = pl.BlockSpec(memory_space=pltpu.HBM)
 
 
-def arrange_kernel(first_ref, a_ref, _, *refs):
-    outs, sems = refs[:-1], refs[-1]
-    copies = []
-    for out, size in zip(outs, PARTS):
-        for n in range(size):
-            t = len(copies)
-            copies.append(pltpu.make_async_copy(a_ref.at[first_ref[0] + t], out.at[n], sems.at[t]))
-            copies[-1].start()
-    for copy in copies:
-        copy.wait()
-
-
-def arrange(first, blocks, before):
-    _, k, side, _ = blocks.shape
-    return pl.pallas_call(
-        arrange_kernel,
-        in_specs=[SMEM, VMEM, ANY],
-        out_specs=[HBM] * len(PARTS),
-        out_shape=[pltpu.HBM((size, k, side, side), blocks.dtype) for size in PARTS],
-        scratch_shapes=[pltpu.SemaphoreType.DMA((sum(PARTS),))],
-        compiler_params=params(6),
-        name="arrange",
-    )(first, blocks, before)
-
-
-def turn_kernel(q_ref, code_ref, qx_ref):
-    rows, width = q_ref.shape
-    qx_ref[0:width, :] = q_ref[...].T
-    qx_ref[width:, :] = jnp.broadcast_to(code_ref[...], (qx_ref.shape[0] - width, rows)).astype(BF16)
+def turn_kernel(q_ref, code_ref, out_ref):
+    side = out_ref.shape[1]
+    down, across = q_ref.shape[1] // side, q_ref.shape[0] // side
+    for i in range(down):
+        for j in range(across):
+            out_ref[i * across + j] = q_ref[j * side : (j + 1) * side, i * side : (i + 1) * side].T
+    out_ref[down * across] = jnp.broadcast_to(code_ref[...], (side, side)).astype(BF16)
 
 
 def turn(q, codes):
-    rows, width = q.shape
+    side = codes.shape[1]
     return pl.pallas_call(
         turn_kernel,
-        out_shape=jax.ShapeDtypeStruct((width + 16, rows), BF16),
+        out_shape=jax.ShapeDtypeStruct((q.size // side**2 + 1, side, side), BF16),
         compiler_params=params(6),
         name="turn",
     )(q, codes)
+
+
+def arrange_kernel(first_ref, a_ref, q_ref, *refs):
+    outs, sems = refs[:-1], refs[-1]
+    k, head = a_ref.shape[1], q_ref.shape[0]
+    copies = [pltpu.make_async_copy(q_ref, outs[0].at[pl.ds(0, head)], sems.at[0])]
+    for j, size in enumerate(PARTS):
+        for n in range(size):
+            t = len(copies)
+            target = outs[j].at[pl.ds((0 if j else head) + n * k, k)]
+            copies.append(pltpu.make_async_copy(a_ref.at[first_ref[0] + t - 1], target, sems.at[t]))
+    for copy in copies:
+        copy.start()
+    for copy in copies:
+        copy.wait()
+
+
+def arrange(first, blocks, q):
+    _, k, side, _ = blocks.shape
+    counts = [size * k + (0 if j else q.shape[0]) for j, size in enumerate(PARTS)]
+    return pl.pallas_call(
+        arrange_kernel,
+        in_specs=[SMEM, VMEM, VMEM],
+        out_specs=[HBM] * len(PARTS),
+        out_shape=[pltpu.HBM((count, side, side), blocks.dtype) for count in counts],
+        scratch_shapes=[pltpu.SemaphoreType.DMA((sum(PARTS) + 1,))],
+        compiler_params=params(6),
+        name="arrange",
+    )(first, blocks, q)
 
 
 def slots_kernel(owners, capacity, owner_ref, _, slot_ref):
@@ -90,26 +97,34 @@
     side = a_ref.shape[2]
     rows = d_ref.shape[1] // 2
     per = rows // side
-    width = c_ref.shape[1]
+    head = 0 if start else q_ref.shape[0]
     d_ref[...] = jnp.zeros(d_ref.shape, d_ref.dtype)
     source = first_ref[0] + start + pl.program_id(0)
-    for base, codes, blk in ((0, mine_ref, a_ref), (rows, theirs_ref, b_ref)):
+    for base, codes in ((0, mine_ref), (rows, theirs_ref)):
         for n in range(k):
             code = codes[source * k + n]
             at_row = pl.multiple_of(base + (code // per) * side, side)
             at_col = pl.multiple_of((code % per) * side, side)
             place = (0, pl.ds(at_row, side), pl.ds(at_col, side))
-            d_ref[place] = (d_ref[place].astype(F32) + blk[0, n].astype(F32)).astype(d_ref.dtype)
-    term = jnp.dot(q_ref[0:width, :], d_ref[0, 0:rows, :], preferred_element_type=F32)
-    term += jnp.dot(qp_ref[0:width, :], d_ref[0, rows:, :], preferred_element_type=F32)
+            block = a_ref[0, n] if base == 0 else b_ref[head + pl.program_id(0) * k + n]
+            d_ref[place] = (d_ref[place].astype(F32) + block.astype(F32)).astype(d_ref.dtype)
+
+    def turned(ref):
+        down = c_ref.shape[1] // side
+        return jnp.concatenate(
+            [jnp.concatenate([ref[i * per + j] for j in range(per)], axis=1) for i in range(down)], axis=0
+        )
+
+    term = jnp.dot(turned(q_ref), d_ref[0, 0:rows, :], preferred_element_type=F32)
+    term += jnp.dot(turned(qp_ref), d_ref[0, rows:, :], preferred_element_type=F32)
     c_ref[0] = term.astype(c_ref.dtype)
 
 
-def strips(start, first, mine, theirs, qx, qx_partner, blocks, received, width, held):
+def strips(start, size, first, mine, theirs, q, opening, blocks, received, shape, held):
     _, k, side, _ = blocks.shape
-    rows = qx.shape[1]
-    size, groups = received.shape[0], sum(PARTS)
-    whole = pl.BlockSpec(qx.shape, lambda i, *_: (0, 0))
+    rows, width = shape
+    groups = sum(PARTS)
+    whole = pl.BlockSpec(q.shape, lambda i, *_: (0, 0, 0))
     return pl.pallas_call(
         functools.partial(strip_kernel, start),
         grid_spec=pltpu.PrefetchScalarGridSpec(
@@ -119,7 +134,7 @@
                 whole,
                 whole,
                 pl.BlockSpec((1, k, side, side), lambda i, first, *_: (first[0] + start + i, 0, 0, 0)),
-                pl.BlockSpec((1, k, side, side), lambda i, *_: (i, 0, 0, 0)),
+                pl.BlockSpec(received.shape, lambda i, *_: (0, 0, 0)),
             ]
             + [HBM] * len(held),
             out_specs=[
@@ -134,7 +149,7 @@
         input_output_aliases={7 + n: n for n in range(len(held))},
         compiler_params=params(10),
         name="strips",
-    )(first, mine, theirs, qx, qx_partner, blocks, received, *held)
+    )(first, mine, theirs, q, opening, blocks, received, *held)
 
 
 def forward_kernel(d_ref, p_ref, own_ref, send_ref, total_ref):
@@ -235,19 +250,18 @@
     halves = [list(range(ring)), list(range(ring, groups))]
 
     codes = (block_row * (n_rows // side) + block_col).reshape(groups * per_group)
-    code_row = jnp.pad(codes.astype(F32), (0, n_rows - codes.shape[0])).reshape(1, n_rows)
-    qx = turn(adjoint_probes, code_row)
-    leaving = arrange(crossing, blocks, qx)
+    code_row = jnp.pad(codes.astype(F32), (0, side - codes.shape[0])).reshape(1, side)
+    q = turn(adjoint_probes, code_row)
+    leaving = arrange(crossing, blocks, q)
     panels = lax.all_gather(probes, "blk", axis=0, tiled=True, axis_index_groups=halves).reshape(ring, n_rows, width)
-    qx_partner = lax.ppermute(qx, "blk", across)
     received = [lax.ppermute(part, "blk", across) for part in leaving]
-    partner_codes = qx_partner[width, 0 : codes.shape[0]].astype(jnp.int32)
+    partner_codes = received[0][q.shape[0] - 1, 0, 0 : codes.shape[0]].astype(jnp.int32)
     slot = slots_of(row_owner.reshape(1, n_rows), owners, capacity, partner_codes)
 
     held = ()
-    for j in range(len(PARTS)):
+    for j, size in enumerate(PARTS):
         held = strips(
-            sum(PARTS[:j]), kept, codes, partner_codes, qx, qx_partner, blocks, received[j], width, held
+            sum(PARTS[:j]), size, kept, codes, partner_codes, q, received[0], blocks, received[j], (n_rows, width), held
         )
     terms, dense = held
     columns = lax.psum_scatter(terms, "blk", scatter_dimension=0, tiled=False, axis_index_groups=halves)

time: 153 us -> 150 us (0.980)
  blocking collectives: 0 us -> 29.9 us
  waiting for transfers between devices: 63.8 us -> 47.5 us
  starting transfers between devices: 40.1 us -> 25.8 us
    all_to_all x0 -> x1, blocking collectives: none -> 29.9 us  [body(): lax.all_to_all(row_packed.reshape(owners, capacity, width), 'grp', 0, 0,...]
    ppermute x3, waiting for transfers between devices: 0.01 us -> 24.2 us  [body(): received = [lax.ppermute(part, 'blk', across) for part in leaving]]
    ppermute x1 -> x0, waiting for transfers between devices: 23.8 us -> none  [body(): qx_partner = lax.ppermute(qx, 'blk', across)]
    reduce_scatter x1, waiting for transfers between devices: 19 us -> 0.61 us  [body(): lax.psum_scatter(terms, 'blk', scatter_dimension=0, tiled=False, axis_ind...]
    all_to_all x1 -> x0, starting transfers between devices: 11.6 us -> none  [body(): lax.all_to_all(row_packed.reshape(owners, capacity, width), 'grp', 0, 0,...]
    ppermute x1 -> x0, starting transfers between devices: 4.93 us -> none  [body(): qx_partner = lax.ppermute(qx, 'blk', across)]
    ppermute x3, starting transfers between devices: 9.9 us -> 12.4 us  [body(): received = [lax.ppermute(part, 'blk', across) for part in leaving]]
    unnamed x13 -> x15, local copies, waits for them, and re-layouts: 7.16 us -> 6.22 us
  transfers between devices with their start and end apart: 9 -> 7, of which waited for: 4 -> 6; matrix products, arithmetic and copies ran while one was open for 3% -> 2% of each run, Pallas kernels for 14% -> 14%
where the time goes in v2:
time: 150 us; the launch traced here: 149 us
  waiting for transfers between devices  47.5 us (32%)
  blocking collectives  29.9 us (20%)
  starting transfers between devices  25.8 us (17%)
  Pallas kernels  22.2 us (15%)
  between operations  14.2 us (9%)
  local copies, waits for them, and re-layouts  6.39 us (4%)
  matrix products  2.09 us (1%)
    all_to_all x1, blocking collectives, body(): lax.all_to_all(row_packed.reshape(owners, capacity, width), 'grp', 0, 0,...  29.9 us
    ppermute x3, waiting for transfers between devices, body(): received = [lax.ppermute(part, 'blk', across) for part in leaving]  24.2 us
    all_to_all x1, waiting for transfers between devices, body(): lax.all_to_all(column_packed.reshape(owners, capacity, width), 'grp', 0,...  16.6 us
    pallas_call x3, Pallas kernels, strips(): pl.pallas_call(functools.partial(strip_kernel, start), grid_spec=pltpu.Pr...  12.7 us
    ppermute x3, starting transfers between devices, body(): received = [lax.ppermute(part, 'blk', across) for part in leaving]  12.4 us
    all_to_all x1, starting transfers between devices, body(): lax.all_to_all(column_packed.reshape(owners, capacity, width), 'grp', 0,...  8.33 us
    unnamed x15, local copies, waits for them, and re-layouts  6.22 us
    pallas_call x1, Pallas kernels, forward(): pl.pallas_call(forward_kernel, grid=(groups // 2,), in_specs=[pl.BlockSpe...  5.84 us
  transfers between devices with their start and end apart: 7, of which 6 were waited for; matrix products, arithmetic and copies ran while one was open for 2% of the time, Pallas kernels for 14%

profile of v2, /device:TPU:24, one launch (start us, length us, event | category | flops | bytes accessed | tf_op | source)
XLA Modules:
  0.0 149.4 jit_solution(6641635206722389168)
XLA Ops:
  7.2 0.7 all-gather.2.cloned.1.call-update
  8.0 0.7 multiply_add_fusion
  8.7 0.1 reshape.40.mine_ref
  8.9 0.9 copy-done.5
  9.8 0.1 turn.1.q_ref
  10.0 1.9 %copy-done = bf16[1,1,16,6,128,128]{5,4,3,2,1,0:T(8,128)(2,1)S(1)} copy-done((bf16[1,1,16,6,128,128]{5,4,3,2,1,0:T(8,128)(2,1)S(1)}, bf16[1,1,16,6,128,128]{5,4,3,2,1,0:T(8,128)(2,1)}, u32[]{:S(2)}) %copy-start) | copy-done | bytes 3145752
  11.9 1.3 arrange.1
  13.2 5.1 %collective-permute-start = (bf16[27,128,128]{2,1,0:T(8,128)(2,1)}, bf16[27,128,128]{2,1,0:T(8,128)(2,1)}, u32[]{:S(2)}, u32[]{:S(2)}) collective-permute-start(bf16[27,128,128]{2,1,0:T(8,128)(2,1)} %get-tuple-element.17), channel_id=1, source_target_pairs={{0,256},{32,288},{64,320},{96,352},{128,384},{160,416},{192,448},{... | collective-permute-start | bytes 2654216 | tf_op jit(solution)/shard_map/ppermute | solution.py:257
  18.2 2.4 %collective-permute-start.2 = (bf16[18,128,128]{2,1,0:T(8,128)(2,1)}, bf16[18,128,128]{2,1,0:T(8,128)(2,1)}, u32[]{:S(2)}, u32[]{:S(2)}) collective-permute-start(bf16[18,128,128]{2,1,0:T(8,128)(2,1)} %get-tuple-element.19), channel_id=1, source_target_pairs={{0,256},{32,288},{64,320},{96,352},{128,384},{160,416},{192,448},{... | collective-permute-start | bytes 1769480 | tf_op jit(solution)/shard_map/ppermute | solution.py:257
  20.7 4.9 %collective-permute-start.1 = (bf16[12,128,128]{2,1,0:T(8,128)(2,1)}, bf16[12,128,128]{2,1,0:T(8,128)(2,1)}, u32[]{:S(2)}, u32[]{:S(2)}) collective-permute-start(bf16[12,128,128]{2,1,0:T(8,128)(2,1)} %get-tuple-element.18), channel_id=1, source_target_pairs={{0,256},{32,288},{64,320},{96,352},{128,384},{160,416},{192,448},{... | collective-permute-start | bytes 1179656 | tf_op jit(solution)/shard_map/ppermute | solution.py:257
  25.6 13.9 %collective-permute-done.qp_ref.b_ref = bf16[27,128,128]{2,1,0:T(8,128)(2,1)} collective-permute-done((bf16[27,128,128]{2,1,0:T(8,128)(2,1)}, bf16[27,128,128]{2,1,0:T(8,128)(2,1)}, u32[]{:S(2)}, u32[]{:S(2)}) %collective-permute-start) | collective-permute-done | bytes 884768 | tf_op jit(solution)/shard_map/ppermute | solution.py:257
  39.6 0.7 fusion.4.theirs_ref._
  40.2 4.6 %strips.3 = (bf16[8,256,512]{2,1,0:T(8,128)(2,1)}, bf16[8,1024,512]{2,1,0:T(8,128)(2,1)}) custom-call(s32[1]{0:T(128)} %bitcast.first_ref, s32[96]{0:T(128)S(1)} %reshape.40.mine_ref, s32[96]{0:T(128)S(1)} %fusion.4.theirs_ref._, bf16[9,128,128]{2,1,0:T(8,128)(2,1)S(1)} %turn.1.q_ref, bf16[27,128,128]{2,1,0:T(8,128)(2,1)} %collective-permute-done.qp_ref.b_ref, ...), custom_call_target="tpu_custom_call" | custom-call | tf_op jit(solution)/shard_map/strips/pallas_call | solution.py:128
  44.8 7.4 %collective-permute-done.2.b_ref = bf16[18,128,128]{2,1,0:T(8,128)(2,1)} collective-permute-done((bf16[18,128,128]{2,1,0:T(8,128)(2,1)}, bf16[18,128,128]{2,1,0:T(8,128)(2,1)}, u32[]{:S(2)}, u32[]{:S(2)}) %collective-permute-start.2) | collective-permute-done | bytes 589856 | tf_op jit(solution)/shard_map/ppermute | solution.py:257
  52.2 4.4 %strips.4 = (bf16[8,256,512]{2,1,0:T(8,128)(2,1)}, bf16[8,1024,512]{2,1,0:T(8,128)(2,1)}) custom-call(s32[1]{0:T(128)} %bitcast.first_ref, s32[96]{0:T(128)S(1)} %reshape.40.mine_ref, s32[96]{0:T(128)S(1)} %fusion.4.theirs_ref._, bf16[9,128,128]{2,1,0:T(8,128)(2,1)S(1)} %turn.1.q_ref, ...), custom_call_target="tpu_custom_call", output_to_operand_aliasing={{0}: (7, {}), {1}: (8, {})} | custom-call | tf_op jit(solution)/shard_map/strips/pallas_call | solution.py:128
  56.6 2.8 %collective-permute-done.1.b_ref = bf16[12,128,128]{2,1,0:T(8,128)(2,1)} collective-permute-done((bf16[12,128,128]{2,1,0:T(8,128)(2,1)}, bf16[12,128,128]{2,1,0:T(8,128)(2,1)}, u32[]{:S(2)}, u32[]{:S(2)}) %collective-permute-start.1) | collective-permute-done | bytes 393248 | tf_op jit(solution)/shard_map/ppermute | solution.py:257
  59.5 3.7 %strips.5 = (bf16[8,256,512]{2,1,0:T(8,128)(2,1)}, bf16[8,1024,512]{2,1,0:T(8,128)(2,1)}) custom-call(s32[1]{0:T(128)} %bitcast.first_ref, s32[96]{0:T(128)S(1)} %reshape.40.mine_ref, s32[96]{0:T(128)S(1)} %fusion.4.theirs_ref._, bf16[9,128,128]{2,1,0:T(8,128)(2,1)S(1)} %turn.1.q_ref, ...), custom_call_target="tpu_custom_call", output_to_operand_aliasing={{0}: (7, {}), {1}: (8, {})} | custom-call | tf_op jit(solution)/shard_map/strips/pallas_call | solution.py:128
  63.2 1.6 %copy-done.2 = bf16[4096,256]{1,0:T(8,128)(2,1)S(1)} copy-done((bf16[4096,256]{1,0:T(8,128)(2,1)S(1)}, bf16[4096,256]{1,0:T(8,128)(2,1)}, u32[]{:S(2)}) %copy-start.2) | copy-done | bytes 2097176
  64.8 5.8 %forward.1 = (f32[512,256]{1,0:T(8,128)S(1)}, bf16[512,256]{1,0:T(8,128)(2,1)S(1)}) custom-call(bf16[8,1024,512]{2,1,0:T(8,128)(2,1)} %get-tuple-element.24.d_ref, bf16[8,512,256]{2,1,0:T(8,128)(2,1)S(1)} %bitcast.43), custom_call_target="tpu_custom_call" | custom-call | tf_op jit(solution)/shard_map/forward/pallas_call | solution.py:177
  70.7 4.9 %collective-permute-start.3 = (bf16[512,256]{1,0:T(8,128)(2,1)S(1)}, bf16[512,256]{1,0:T(8,128)(2,1)S(1)}, u32[]{:S(2)}, u32[]{:S(2)}) collective-permute-start(bf16[512,256]{1,0:T(8,128)(2,1)S(1)} %get-tuple-element.26), channel_id=1, source_target_pairs={{0,256},{32,288},{64,320},{96,352},{128,384},{160,416},{192,448},{... | collective-permute-start | bytes 786440 | tf_op jit(solution)/shard_map/ppermute | solution.py:269
  75.6 0.2 slots.1.slot_ref
  75.8 5.4 %collective-permute-done.3.got_ref = bf16[512,256]{1,0:T(8,128)(2,1)S(1)} collective-permute-done((bf16[512,256]{1,0:T(8,128)(2,1)S(1)}, bf16[512,256]{1,0:T(8,128)(2,1)S(1)}, u32[]{:S(2)}, u32[]{:S(2)}) %collective-permute-start.3) | collective-permute-done | bytes 262176 | tf_op jit(solution)/shard_map/ppermute | solution.py:269
  81.2 0.8 pack_rows.1
  82.0 29.9 %all_to_all.10._ = bf16[32,32,256]{2,1,0:T(8,128)(2,1)S(1)} all-to-all(bf16[32,32,256]{2,1,0:T(8,128)(2,1)S(1)} %bitcast.46), channel_id=1, replica_groups=mesh['blk'=16,'grp'=32] {'grp'}, dimensions={0} | all-to-all | bytes 1048576 | tf_op jit(solution)/shard_map/all_to_all | solution.py:271
  111.9 0.6 reduce-scatter.2.cloned.1.call-done
  112.5 0.9 copy-done.3
  113.4 1.3 pack_columns.1
  114.7 8.3 %all-to-all-start.1 = ((bf16[32,32,256]{2,1,0:T(8,128)(2,1)}), bf16[32,32,256]{2,1,0:T(8,128)(2,1)S(1)}, u32[]{:S(2)}, u32[]{:S(2)}) async-start(bf16[32,32,256]{2,1,0:T(8,128)(2,1)} %bitcast.13), calls=%async_computation.2 | async-start | bytes 1048576 | tf_op jit(solution)/shard_map/all_to_all | solution.py:273
  123.1 1.0 fusion.2
  124.1 0.8 copy.17
  124.9 16.6 %all-to-all-done.1 = bf16[32,32,256]{2,1,0:T(8,128)(2,1)S(1)} async-done(((bf16[32,32,256]{2,1,0:T(8,128)(2,1)}), bf16[32,32,256]{2,1,0:T(8,128)(2,1)S(1)}, u32[]{:S(2)}, u32[]{:S(2)}) %all-to-all-start.1) | async-done | bytes 524320 | tf_op jit(solution)/shard_map/all_to_all | solution.py:273
  141.5 1.0 fusion.3
  (17 shorter events, 0.2 us)
Async XLA Ops:
  7.2 56.1 %all-gather.2.cloned.1.call-start = ((), (), s32[]{:S(2)}) async-start(), calls=%async_computation.3 | async-start | bytes 2359296 | tf_op jit(solution)/shard_map/all_gather | solution.py:256
  7.9 104.6 %reduce-scatter.2.cloned.1.call-start = ((), (), s32[]{:S(2)}) async-start(), calls=%async_computation.4 | async-start | bytes 2359296 | tf_op jit(solution)/shard_map/reduce_scatter | solution.py:267
  8.9 1.0 copy-start.5
  10.0 1.9 %copy-start = (bf16[1,1,16,6,128,128]{5,4,3,2,1,0:T(8,128)(2,1)S(1)}, bf16[1,1,16,6,128,128]{5,4,3,2,1,0:T(8,128)(2,1)}, u32[]{:S(2)}) copy-start(bf16[1,1,16,6,128,128]{5,4,3,2,1,0:T(8,128)(2,1)} %param.6) | copy-start | bytes 9437188
  11.9 28.4 %copy-start.1 = (bf16[1,1,16,6,128,128]{5,4,3,2,1,0:T(8,128)(2,1)S(1)}, bf16[1,1,16,6,128,128]{5,4,3,2,1,0:T(8,128)(2,1)}, u32[]{:S(2)}) copy-start(bf16[1,1,16,6,128,128]{5,4,3,2,1,0:T(8,128)(2,1)} %param.6) | copy-start | bytes 9437188
  13.2 26.4 %collective-permute-start = (bf16[27,128,128]{2,1,0:T(8,128)(2,1)}, bf16[27,128,128]{2,1,0:T(8,128)(2,1)}, u32[]{:S(2)}, u32[]{:S(2)}) collective-permute-start(bf16[27,128,128]{2,1,0:T(8,128)(2,1)} %get-tuple-element.17), channel_id=1, source_target_pairs={{0,256},{32,288},{64,320},{96,352},{128,384},{160,416},{192,448},{... | collective-permute-start | bytes 2654216 | tf_op jit(solution)/shard_map/ppermute | solution.py:257
  18.2 33.9 %collective-permute-start.2 = (bf16[18,128,128]{2,1,0:T(8,128)(2,1)}, bf16[18,128,128]{2,1,0:T(8,128)(2,1)}, u32[]{:S(2)}, u32[]{:S(2)}) collective-permute-start(bf16[18,128,128]{2,1,0:T(8,128)(2,1)} %get-tuple-element.19), channel_id=1, source_target_pairs={{0,256},{32,288},{64,320},{96,352},{128,384},{160,416},{192,448},{... | collective-permute-start | bytes 1769480 | tf_op jit(solution)/shard_map/ppermute | solution.py:257
  20.7 38.8 %collective-permute-start.1 = (bf16[12,128,128]{2,1,0:T(8,128)(2,1)}, bf16[12,128,128]{2,1,0:T(8,128)(2,1)}, u32[]{:S(2)}, u32[]{:S(2)}) collective-permute-start(bf16[12,128,128]{2,1,0:T(8,128)(2,1)} %get-tuple-element.18), channel_id=1, source_target_pairs={{0,256},{32,288},{64,320},{96,352},{128,384},{160,416},{192,448},{... | collective-permute-start | bytes 1179656 | tf_op jit(solution)/shard_map/ppermute | solution.py:257
  63.2 1.6 %copy-start.2 = (bf16[4096,256]{1,0:T(8,128)(2,1)S(1)}, bf16[4096,256]{1,0:T(8,128)(2,1)}, u32[]{:S(2)}) copy-start(bf16[4096,256]{1,0:T(8,128)(2,1)} %all-gather.2.cloned.1.call-done) | copy-start | bytes 6291460
  64.8 10.8 %copy-start.6 = (s32[512,1]{0,1:T(1,128)S(1)}, s32[512,1]{0,1:T(1,128)}, u32[]{:S(2)}) copy-start(s32[512,1]{0,1:T(1,128)} %param.11) | copy-start | bytes 6148
  70.7 10.6 %collective-permute-start.3 = (bf16[512,256]{1,0:T(8,128)(2,1)S(1)}, bf16[512,256]{1,0:T(8,128)(2,1)S(1)}, u32[]{:S(2)}, u32[]{:S(2)}) collective-permute-start(bf16[512,256]{1,0:T(8,128)(2,1)S(1)} %get-tuple-element.26), channel_id=1, source_target_pairs={{0,256},{32,288},{64,320},{96,352},{128,384},{160,416},{192,448},{... | collective-permute-start | bytes 786440 | tf_op jit(solution)/shard_map/ppermute | solution.py:269
  112.5 0.9 copy-start.3
  113.4 10.7 %copy-start.4 = (bf16[1,256,512]{2,1,0:T(8,128)(2,1)S(1)}, bf16[1,256,512]{2,1,0:T(8,128)(2,1)}, u32[]{:S(2)}) copy-start(bf16[1,256,512]{2,1,0:T(8,128)(2,1)} %reduce-scatter.2.cloned.1.call-done) | copy-start | bytes 786436
  114.7 26.8 %all-to-all-start.1 = ((bf16[32,32,256]{2,1,0:T(8,128)(2,1)}), bf16[32,32,256]{2,1,0:T(8,128)(2,1)S(1)}, u32[]{:S(2)}, u32[]{:S(2)}) async-start(bf16[32,32,256]{2,1,0:T(8,128)(2,1)} %bitcast.13), calls=%async_computation.2 | async-start | bytes 1048576 | tf_op jit(solution)/shard_map/all_to_all | solution.py:273
Sparse Core Ops, SparseCore 0:
  10.1 47.3 all-gather.1
  63.3 49.1 reduce-scatter.1

commit v3 on v2

--- a/solution.py
+++ b/solution.py
@@ -9,7 +9,7 @@
 
 F32 = jnp.float32
 BF16 = jnp.bfloat16
-PARTS = (3, 3, 2)
+PARTS = (3, 3, 1, 1)
 
 
 def params(mib):
@@ -22,52 +22,59 @@
 HBM = pl.BlockSpec(memory_space=pltpu.HBM)
 
 
-def turn_kernel(q_ref, code_ref, out_ref):
-    side = out_ref.shape[1]
-    down, across = q_ref.shape[1] // side, q_ref.shape[0] // side
+def prepare_kernel(first_ref, a_ref, q_ref, code_ref, own_ref, *refs):
+    outs, (a_buf, q_buf, in_sems, out_sems) = refs[:-4], refs[-4:]
+    k, side = a_buf.shape[1:3]
+    head, groups = own_ref.shape[0], a_buf.shape[0]
+    q_in = pltpu.make_async_copy(q_ref, q_buf, in_sems.at[groups])
+    a_in = [pltpu.make_async_copy(a_ref.at[first_ref[0] + t], a_buf.at[t], in_sems.at[t]) for t in range(groups)]
+    for copy in [q_in] + a_in:
+        copy.start()
+    q_in.wait()
+    down, across = q_buf.shape[1] // side, q_buf.shape[0] // side
     for i in range(down):
         for j in range(across):
-            out_ref[i * across + j] = q_ref[j * side : (j + 1) * side, i * side : (i + 1) * side].T
-    out_ref[down * across] = jnp.broadcast_to(code_ref[...], (side, side)).astype(BF16)
-
-
-def turn(q, codes):
-    side = codes.shape[1]
-    return pl.pallas_call(
-        turn_kernel,
-        out_shape=jax.ShapeDtypeStruct((q.size // side**2 + 1, side, side), BF16),
-        compiler_params=params(6),
-        name="turn",
-    )(q, codes)
-
-
-def arrange_kernel(first_ref, a_ref, q_ref, *refs):
-    outs, sems = refs[:-1], refs[-1]
-    k, head = a_ref.shape[1], q_ref.shape[0]
-    copies = [pltpu.make_async_copy(q_ref, outs[0].at[pl.ds(0, head)], sems.at[0])]
+            own_ref[i * across + j] = q_buf[j * side : (j + 1) * side, i * side : (i + 1) * side].T
+    own_ref[down * across] = jnp.broadcast_to(code_ref[...], (side, side)).astype(BF16)
+    copies = [pltpu.make_async_copy(own_ref, outs[0].at[pl.ds(0, head)], out_sems.at[groups])]
+    copies[0].start()
+    t = 0
     for j, size in enumerate(PARTS):
         for n in range(size):
-            t = len(copies)
+            a_in[t].wait()
             target = outs[j].at[pl.ds((0 if j else head) + n * k, k)]
-            copies.append(pltpu.make_async_copy(a_ref.at[first_ref[0] + t - 1], target, sems.at[t]))
-    for copy in copies:
-        copy.start()
+            copies.append(pltpu.make_async_copy(a_buf.at[t], target, out_sems.at[t]))
+            copies[-1].start()
+            t += 1
     for copy in copies:
         copy.wait()
 
 
-def arrange(first, blocks, q):
+def prepare(first, blocks, q, codes):
     _, k, side, _ = blocks.shape
-    counts = [size * k + (0 if j else q.shape[0]) for j, size in enumerate(PARTS)]
-    return pl.pallas_call(
-        arrange_kernel,
-        in_specs=[SMEM, VMEM, VMEM],
-        out_specs=[HBM] * len(PARTS),
-        out_shape=[pltpu.HBM((count, side, side), blocks.dtype) for count in counts],
-        scratch_shapes=[pltpu.SemaphoreType.DMA((sum(PARTS) + 1,))],
-        compiler_params=params(6),
-        name="arrange",
-    )(first, blocks, q)
+    head, groups = q.size // side**2 + 1, sum(PARTS)
+    counts = [size * k + (0 if j else head) for j, size in enumerate(PARTS)]
+    found = pl.pallas_call(
+        prepare_kernel,
+        in_specs=[SMEM, HBM, HBM, VMEM],
+        out_specs=[VMEM] + [HBM] * len(PARTS),
+        out_shape=[jax.ShapeDtypeStruct((head, side, side), BF16)]
+        + [pltpu.HBM((count, side, side), blocks.dtype) for count in counts],
+        scratch_shapes=[
+            pltpu.VMEM((groups, k, side, side), blocks.dtype),
+            pltpu.VMEM(q.shape, q.dtype),
+            pltpu.SemaphoreType.DMA((groups + 1,)),
+            pltpu.SemaphoreType.DMA((groups + 1,)),
+        ],
+        compiler_params=params(8),
+        name="prepare",
+    )(
+        first,
+        pltpu.with_memory_space_constraint(blocks, pltpu.HBM),
+        pltpu.with_memory_space_constraint(q, pltpu.HBM),
+        codes,
+    )
+    return found[0], found[1:]
 
 
 def slots_kernel(owners, capacity, owner_ref, _, slot_ref):
@@ -251,8 +258,7 @@
 
     codes = (block_row * (n_rows // side) + block_col).reshape(groups * per_group)
     code_row = jnp.pad(codes.astype(F32), (0, side - codes.shape[0])).reshape(1, side)
-    q = turn(adjoint_probes, code_row)
-    leaving = arrange(crossing, blocks, q)
+    q, leaving = prepare(crossing, blocks, adjoint_probes, code_row)
     panels = lax.all_gather(probes, "blk", axis=0, tiled=True, axis_index_groups=halves).reshape(ring, n_rows, width)
     received = [lax.ppermute(part, "blk", across) for part in leaving]
     partner_codes = received[0][q.shape[0] - 1, 0, 0 : codes.shape[0]].astype(jnp.int32)

time: 150 us -> 151 us (level)
  Pallas kernels: 22.2 us -> 25.4 us
  local copies, waits for them, and re-layouts: 6.39 us -> 3.56 us
  waiting for transfers between devices: 47.5 us -> 44.9 us
  starting transfers between devices: 25.8 us -> 28.4 us
    unnamed x15 -> x11, local copies, waits for them, and re-layouts: 6.22 us -> 3.39 us
    ppermute x3 -> x4, waiting for transfers between devices: 24.2 us -> 21.7 us  [body(): received = [lax.ppermute(part, 'blk', across) for part in leaving]]
    ppermute x3 -> x4, starting transfers between devices: 12.4 us -> 14.7 us  [body(): received = [lax.ppermute(part, 'blk', across) for part in leaving]]
    pallas_call x3 -> x4, Pallas kernels: 12.7 us -> 14.9 us  [strips(): pl.pallas_call(functools.partial(strip_kernel, start), grid_spec=pltpu.Pr...]
  transfers between devices with their start and end apart: 7 -> 8, of which waited for: 6 -> 6; matrix products, arithmetic and copies ran while one was open for 2% -> 2% of each run, Pallas kernels for 14% -> 16%
where the time goes in v3:
time: 151 us; the launch traced here: 150 us
  waiting for transfers between devices  44.9 us (30%)
  blocking collectives  29.9 us (20%)
  starting transfers between devices  28.4 us (19%)
  Pallas kernels  25.4 us (17%)
  between operations  14.2 us (9%)
  local copies, waits for them, and re-layouts  3.56 us (2%)
  matrix products  2.09 us (1%)
  other arithmetic  1.53 us (1%)
    all_to_all x1, blocking collectives, body(): lax.all_to_all(row_packed.reshape(owners, capacity, width), 'grp', 0, 0,...  29.9 us
    ppermute x4, waiting for transfers between devices, body(): received = [lax.ppermute(part, 'blk', across) for part in leaving]  21.7 us
    all_to_all x1, waiting for transfers between devices, body(): lax.all_to_all(column_packed.reshape(owners, capacity, width), 'grp', 0,...  16.6 us
    pallas_call x4, Pallas kernels, strips(): pl.pallas_call(functools.partial(strip_kernel, start), grid_spec=pltpu.Pr...  14.9 us
    ppermute x4, starting transfers between devices, body(): received = [lax.ppermute(part, 'blk', across) for part in leaving]  14.7 us
    all_to_all x1, starting transfers between devices, body(): lax.all_to_all(column_packed.reshape(owners, capacity, width), 'grp', 0,...  8.66 us
    pallas_call x1, Pallas kernels, forward(): pl.pallas_call(forward_kernel, grid=(groups // 2,), in_specs=[pl.BlockSpe...  5.84 us
    ppermute x1, waiting for transfers between devices, body(): got = lax.ppermute(partial, 'blk', across)  5.41 us
  transfers between devices with their start and end apart: 8, of which 6 were waited for; matrix products, arithmetic and copies ran while one was open for 2% of the time, Pallas kernels for 16%

profile of v3, /device:TPU:24, one launch (start us, length us, event | category | flops | bytes accessed | tf_op | source)
XLA Modules:
  0.0 150.0 jit_solution(4275790797501817129)
XLA Ops:
  7.2 0.7 all-gather.2.cloned.1.call-update
  8.0 0.9 multiply_add_fusion
  8.8 0.1 copy.18
  8.9 0.1 reshape.40.mine_ref
  9.0 2.5 %prepare.1 = (bf16[9,128,128]{2,1,0:T(8,128)(2,1)S(1)}, bf16[27,128,128]{2,1,0:T(8,128)(2,1)}, bf16[18,128,128]{2,1,0:T(8,128)(2,1)}, bf16[6,128,128]{2,1,0:T(8,128)(2,1)}, bf16[6,128,128]{2,1,0:T(8,128)(2,1)}) custom-call(s32[1]{0:T(128)} %bitcast.1.first_ref, bf16[16,6,128,128]{3,2,1,0:T(8,128)(2,1)} %bitcast.39, bf16[512,256]{1,0:T(8,128)(2,1)} %q_ref.1, ...), custom_call_target="tpu_custom_call" | custom-call | tf_op jit(solution)/shard_map/prepare/pallas_call | solution.py:57
  11.5 4.9 %collective-permute-start = (bf16[27,128,128]{2,1,0:T(8,128)(2,1)}, bf16[27,128,128]{2,1,0:T(8,128)(2,1)}, u32[]{:S(2)}, u32[]{:S(2)}) collective-permute-start(bf16[27,128,128]{2,1,0:T(8,128)(2,1)} %get-tuple-element.21), channel_id=1, source_target_pairs={{0,256},{32,288},{64,320},{96,352},{128,384},{160,416},{192,448},{... | collective-permute-start | bytes 2654216 | tf_op jit(solution)/shard_map/ppermute | solution.py:263
  16.4 2.4 %collective-permute-start.3 = (bf16[18,128,128]{2,1,0:T(8,128)(2,1)}, bf16[18,128,128]{2,1,0:T(8,128)(2,1)}, u32[]{:S(2)}, u32[]{:S(2)}) collective-permute-start(bf16[18,128,128]{2,1,0:T(8,128)(2,1)} %get-tuple-element.25), channel_id=1, source_target_pairs={{0,256},{32,288},{64,320},{96,352},{128,384},{160,416},{192,448},{... | collective-permute-start | bytes 1769480 | tf_op jit(solution)/shard_map/ppermute | solution.py:263
  18.9 4.9 %collective-permute-start.1 = (bf16[6,128,128]{2,1,0:T(8,128)(2,1)}, bf16[6,128,128]{2,1,0:T(8,128)(2,1)}, u32[]{:S(2)}, u32[]{:S(2)}) collective-permute-start(bf16[6,128,128]{2,1,0:T(8,128)(2,1)} %get-tuple-element.23), channel_id=1, source_target_pairs={{0,256},{32,288},{64,320},{96,352},{128,384},{160,416},{192,448},{... | collective-permute-start | bytes 589832 | tf_op jit(solution)/shard_map/ppermute | solution.py:263
  23.8 2.4 %collective-permute-start.2 = (bf16[6,128,128]{2,1,0:T(8,128)(2,1)}, bf16[6,128,128]{2,1,0:T(8,128)(2,1)}, u32[]{:S(2)}, u32[]{:S(2)}) collective-permute-start(bf16[6,128,128]{2,1,0:T(8,128)(2,1)} %get-tuple-element.24), channel_id=1, source_target_pairs={{0,256},{32,288},{64,320},{96,352},{128,384},{160,416},{192,448},{... | collective-permute-start | bytes 589832 | tf_op jit(solution)/shard_map/ppermute | solution.py:263
  26.2 11.5 %collective-permute-done.qp_ref.b_ref = bf16[27,128,128]{2,1,0:T(8,128)(2,1)} collective-permute-done((bf16[27,128,128]{2,1,0:T(8,128)(2,1)}, bf16[27,128,128]{2,1,0:T(8,128)(2,1)}, u32[]{:S(2)}, u32[]{:S(2)}) %collective-permute-start) | collective-permute-done | bytes 884768 | tf_op jit(solution)/shard_map/ppermute | solution.py:263
  37.8 0.7 fusion.4.theirs_ref._
  38.4 4.6 %strips.4 = (bf16[8,256,512]{2,1,0:T(8,128)(2,1)}, bf16[8,1024,512]{2,1,0:T(8,128)(2,1)}) custom-call(s32[1]{0:T(128)} %bitcast.first_ref, s32[96]{0:T(128)S(1)} %reshape.40.mine_ref, s32[96]{0:T(128)S(1)} %fusion.4.theirs_ref._, bf16[9,128,128]{2,1,0:T(8,128)(2,1)S(1)} %get-tuple-element.22.q_ref, bf16[27,128,128]{2,1,0:T(8,128)(2,1)} %collective-permute-done.qp_ref.b_ref, ...), custom_call_target="tpu_custom_call" | custom-call | tf_op jit(solution)/shard_map/strips/pallas_call | solution.py:135
  43.0 7.4 %collective-permute-done.3.b_ref = bf16[18,128,128]{2,1,0:T(8,128)(2,1)} collective-permute-done((bf16[18,128,128]{2,1,0:T(8,128)(2,1)}, bf16[18,128,128]{2,1,0:T(8,128)(2,1)}, u32[]{:S(2)}, u32[]{:S(2)}) %collective-permute-start.3) | collective-permute-done | bytes 589856 | tf_op jit(solution)/shard_map/ppermute | solution.py:263
  50.4 4.4 %strips.5 = (bf16[8,256,512]{2,1,0:T(8,128)(2,1)}, bf16[8,1024,512]{2,1,0:T(8,128)(2,1)}) custom-call(s32[1]{0:T(128)} %bitcast.first_ref, s32[96]{0:T(128)S(1)} %reshape.40.mine_ref, s32[96]{0:T(128)S(1)} %fusion.4.theirs_ref._, bf16[9,128,128]{2,1,0:T(8,128)(2,1)S(1)} %get-tuple-element.22.q_ref, ...), custom_call_target="tpu_custom_call", output_to_operand_aliasing={{0}: (7, {}), {1}: (8, {})} | custom-call | tf_op jit(solution)/shard_map/strips/pallas_call | solution.py:135
  54.8 2.8 %collective-permute-done.2.b_ref = bf16[6,128,128]{2,1,0:T(8,128)(2,1)} collective-permute-done((bf16[6,128,128]{2,1,0:T(8,128)(2,1)}, bf16[6,128,128]{2,1,0:T(8,128)(2,1)}, u32[]{:S(2)}, u32[]{:S(2)}) %collective-permute-start.2) | collective-permute-done | bytes 196640 | tf_op jit(solution)/shard_map/ppermute | solution.py:263
  57.7 2.9 %strips.6 = (bf16[8,256,512]{2,1,0:T(8,128)(2,1)}, bf16[8,1024,512]{2,1,0:T(8,128)(2,1)}) custom-call(s32[1]{0:T(128)} %bitcast.first_ref, s32[96]{0:T(128)S(1)} %reshape.40.mine_ref, s32[96]{0:T(128)S(1)} %fusion.4.theirs_ref._, bf16[9,128,128]{2,1,0:T(8,128)(2,1)S(1)} %get-tuple-element.22.q_ref, ...), custom_call_target="tpu_custom_call", output_to_operand_aliasing={{0}: (7, {}), {1}: (8, {})} | custom-call | tf_op jit(solution)/shard_map/strips/pallas_call | solution.py:135
  60.6 2.9 %strips.7 = (bf16[8,256,512]{2,1,0:T(8,128)(2,1)}, bf16[8,1024,512]{2,1,0:T(8,128)(2,1)}) custom-call(s32[1]{0:T(128)} %bitcast.first_ref, s32[96]{0:T(128)S(1)} %reshape.40.mine_ref, s32[96]{0:T(128)S(1)} %fusion.4.theirs_ref._, bf16[9,128,128]{2,1,0:T(8,128)(2,1)S(1)} %get-tuple-element.22.q_ref, ...), custom_call_target="tpu_custom_call", output_to_operand_aliasing={{0}: (7, {}), {1}: (8, {})} | custom-call | tf_op jit(solution)/shard_map/strips/pallas_call | solution.py:135
  63.6 1.6 %copy-done.1 = bf16[4096,256]{1,0:T(8,128)(2,1)S(1)} copy-done((bf16[4096,256]{1,0:T(8,128)(2,1)S(1)}, bf16[4096,256]{1,0:T(8,128)(2,1)}, u32[]{:S(2)}) %copy-start.1) | copy-done | bytes 2097176
  65.2 5.8 %forward.1 = (f32[512,256]{1,0:T(8,128)S(1)}, bf16[512,256]{1,0:T(8,128)(2,1)S(1)}) custom-call(bf16[8,1024,512]{2,1,0:T(8,128)(2,1)} %get-tuple-element.32.d_ref, bf16[8,512,256]{2,1,0:T(8,128)(2,1)S(1)} %bitcast.44), custom_call_target="tpu_custom_call" | custom-call | tf_op jit(solution)/shard_map/forward/pallas_call | solution.py:184
  71.0 4.9 %collective-permute-start.4 = (bf16[512,256]{1,0:T(8,128)(2,1)S(1)}, bf16[512,256]{1,0:T(8,128)(2,1)S(1)}, u32[]{:S(2)}, u32[]{:S(2)}) collective-permute-start(bf16[512,256]{1,0:T(8,128)(2,1)S(1)} %get-tuple-element.34), channel_id=1, source_target_pairs={{0,256},{32,288},{64,320},{96,352},{128,384},{160,416},{192,448},{... | collective-permute-start | bytes 786440 | tf_op jit(solution)/shard_map/ppermute | solution.py:275
  76.0 0.2 slots.1.slot_ref
  76.2 5.4 %collective-permute-done.4.got_ref = bf16[512,256]{1,0:T(8,128)(2,1)S(1)} collective-permute-done((bf16[512,256]{1,0:T(8,128)(2,1)S(1)}, bf16[512,256]{1,0:T(8,128)(2,1)S(1)}, u32[]{:S(2)}, u32[]{:S(2)}) %collective-permute-start.4) | collective-permute-done | bytes 262176 | tf_op jit(solution)/shard_map/ppermute | solution.py:275
  81.6 0.8 pack_rows.1
  82.4 29.9 %all_to_all.10._ = bf16[32,32,256]{2,1,0:T(8,128)(2,1)S(1)} all-to-all(bf16[32,32,256]{2,1,0:T(8,128)(2,1)S(1)} %bitcast.47), channel_id=1, replica_groups=mesh['blk'=16,'grp'=32] {'grp'}, dimensions={0} | all-to-all | bytes 1048576 | tf_op jit(solution)/shard_map/all_to_all | solution.py:277
  112.2 0.5 reduce-scatter.2.cloned.1.call-done
  112.7 0.9 copy-done.2
  113.7 1.3 pack_columns.1
  115.0 8.7 %all-to-all-start.1 = ((bf16[32,32,256]{2,1,0:T(8,128)(2,1)}), bf16[32,32,256]{2,1,0:T(8,128)(2,1)S(1)}, u32[]{:S(2)}, u32[]{:S(2)}) async-start(bf16[32,32,256]{2,1,0:T(8,128)(2,1)} %bitcast.13), calls=%async_computation.2 | async-start | bytes 1048576 | tf_op jit(solution)/shard_map/all_to_all | solution.py:279
  123.6 1.0 fusion.2
  124.7 0.8 copy.19
  125.5 16.6 %all-to-all-done.1 = bf16[32,32,256]{2,1,0:T(8,128)(2,1)S(1)} async-done(((bf16[32,32,256]{2,1,0:T(8,128)(2,1)}), bf16[32,32,256]{2,1,0:T(8,128)(2,1)S(1)}, u32[]{:S(2)}, u32[]{:S(2)}) %all-to-all-start.1) | async-done | bytes 524320 | tf_op jit(solution)/shard_map/all_to_all | solution.py:279
  142.1 1.0 fusion.3
  (15 shorter events, 0.1 us)
Async XLA Ops:
  7.2 31.3 %copy-start = (bf16[1,1,16,6,128,128]{5,4,3,2,1,0:T(8,128)(2,1)S(1)}, bf16[1,1,16,6,128,128]{5,4,3,2,1,0:T(8,128)(2,1)}, u32[]{:S(2)}) copy-start(bf16[1,1,16,6,128,128]{5,4,3,2,1,0:T(8,128)(2,1)} %param.6) | copy-start | bytes 9437188
  7.2 56.4 %all-gather.2.cloned.1.call-start = ((), (), s32[]{:S(2)}) async-start(), calls=%async_computation.3 | async-start | bytes 2359296 | tf_op jit(solution)/shard_map/all_gather | solution.py:262
  7.9 104.8 %reduce-scatter.2.cloned.1.call-start = ((), (), s32[]{:S(2)}) async-start(), calls=%async_computation.4 | async-start | bytes 2359296 | tf_op jit(solution)/shard_map/reduce_scatter | solution.py:273
  11.5 26.2 %collective-permute-start = (bf16[27,128,128]{2,1,0:T(8,128)(2,1)}, bf16[27,128,128]{2,1,0:T(8,128)(2,1)}, u32[]{:S(2)}, u32[]{:S(2)}) collective-permute-start(bf16[27,128,128]{2,1,0:T(8,128)(2,1)} %get-tuple-element.21), channel_id=1, source_target_pairs={{0,256},{32,288},{64,320},{96,352},{128,384},{160,416},{192,448},{... | collective-permute-start | bytes 2654216 | tf_op jit(solution)/shard_map/ppermute | solution.py:263
  16.4 33.9 %collective-permute-start.3 = (bf16[18,128,128]{2,1,0:T(8,128)(2,1)}, bf16[18,128,128]{2,1,0:T(8,128)(2,1)}, u32[]{:S(2)}, u32[]{:S(2)}) collective-permute-start(bf16[18,128,128]{2,1,0:T(8,128)(2,1)} %get-tuple-element.25), channel_id=1, source_target_pairs={{0,256},{32,288},{64,320},{96,352},{128,384},{160,416},{192,448},{... | collective-permute-start | bytes 1769480 | tf_op jit(solution)/shard_map/ppermute | solution.py:263
  18.9 41.7 %collective-permute-start.1 = (bf16[6,128,128]{2,1,0:T(8,128)(2,1)}, bf16[6,128,128]{2,1,0:T(8,128)(2,1)}, u32[]{:S(2)}, u32[]{:S(2)}) collective-permute-start(bf16[6,128,128]{2,1,0:T(8,128)(2,1)} %get-tuple-element.23), channel_id=1, source_target_pairs={{0,256},{32,288},{64,320},{96,352},{128,384},{160,416},{192,448},{... | collective-permute-start | bytes 589832 | tf_op jit(solution)/shard_map/ppermute | solution.py:263
  23.8 33.9 %collective-permute-start.2 = (bf16[6,128,128]{2,1,0:T(8,128)(2,1)}, bf16[6,128,128]{2,1,0:T(8,128)(2,1)}, u32[]{:S(2)}, u32[]{:S(2)}) collective-permute-start(bf16[6,128,128]{2,1,0:T(8,128)(2,1)} %get-tuple-element.24), channel_id=1, source_target_pairs={{0,256},{32,288},{64,320},{96,352},{128,384},{160,416},{192,448},{... | collective-permute-start | bytes 589832 | tf_op jit(solution)/shard_map/ppermute | solution.py:263
  63.6 1.6 %copy-start.1 = (bf16[4096,256]{1,0:T(8,128)(2,1)S(1)}, bf16[4096,256]{1,0:T(8,128)(2,1)}, u32[]{:S(2)}) copy-start(bf16[4096,256]{1,0:T(8,128)(2,1)} %all-gather.2.cloned.1.call-done) | copy-start | bytes 6291460
  65.2 10.8 %copy-start.4 = (s32[512,1]{0,1:T(1,128)S(1)}, s32[512,1]{0,1:T(1,128)}, u32[]{:S(2)}) copy-start(s32[512,1]{0,1:T(1,128)} %param.11) | copy-start | bytes 6148
  71.0 10.6 %collective-permute-start.4 = (bf16[512,256]{1,0:T(8,128)(2,1)S(1)}, bf16[512,256]{1,0:T(8,128)(2,1)S(1)}, u32[]{:S(2)}, u32[]{:S(2)}) collective-permute-start(bf16[512,256]{1,0:T(8,128)(2,1)S(1)} %get-tuple-element.34), channel_id=1, source_target_pairs={{0,256},{32,288},{64,320},{96,352},{128,384},{160,416},{192,448},{... | collective-permute-start | bytes 786440 | tf_op jit(solution)/shard_map/ppermute | solution.py:275
  112.7 0.9 copy-start.2
  113.7 11.0 %copy-start.3 = (bf16[1,256,512]{2,1,0:T(8,128)(2,1)S(1)}, bf16[1,256,512]{2,1,0:T(8,128)(2,1)}, u32[]{:S(2)}) copy-start(bf16[1,256,512]{2,1,0:T(8,128)(2,1)} %reduce-scatter.2.cloned.1.call-done) | copy-start | bytes 786436
  115.0 27.1 %all-to-all-start.1 = ((bf16[32,32,256]{2,1,0:T(8,128)(2,1)}), bf16[32,32,256]{2,1,0:T(8,128)(2,1)S(1)}, u32[]{:S(2)}, u32[]{:S(2)}) async-start(bf16[32,32,256]{2,1,0:T(8,128)(2,1)} %bitcast.13), calls=%async_computation.2 | async-start | bytes 1048576 | tf_op jit(solution)/shard_map/all_to_all | solution.py:279
Sparse Core Ops, SparseCore 0:
  10.1 47.4 all-gather.1
  63.7 49.0 reduce-scatter.1

commit v4 on v3

--- a/solution.py
+++ b/solution.py
@@ -159,9 +159,8 @@
     )(first, mine, theirs, q, opening, blocks, received, *held)
 
 
-def forward_kernel(d_ref, p_ref, own_ref, send_ref, total_ref):
+def forward_kernel(d_ref, p_ref, _, out_ref, total_ref):
     step = pl.program_id(0)
-    rows = own_ref.shape[0]
     term = sum(jnp.dot(d_ref[n], p_ref[n], preferred_element_type=F32) for n in range(d_ref.shape[0]))
 
     @pl.when(step == 0)
@@ -174,26 +173,25 @@
 
     @pl.when(step == pl.num_programs(0) - 1)
     def _():
-        own_ref[...] = total_ref[0:rows, :]
-        send_ref[...] = total_ref[rows:, :].astype(send_ref.dtype)
-
-
-def forward(dense, panels):
+        out_ref[...] = total_ref[...].astype(out_ref.dtype)
+
+
+def forward(dense, panels, half, dtype, before):
     groups, rows, width = panels.shape
-    whole = pl.BlockSpec((rows, width), lambda i: (0, 0))
     return pl.pallas_call(
         forward_kernel,
         grid=(groups // 2,),
         in_specs=[
-            pl.BlockSpec((2, 2 * rows, rows), lambda i: (i, 0, 0)),
+            pl.BlockSpec((2, rows, rows), lambda i: (i, half, 0)),
             pl.BlockSpec((2, rows, width), lambda i: (i, 0, 0)),
+            ANY,
         ],
-        out_specs=[whole, whole],
-        scratch_shapes=[pltpu.VMEM((2 * rows, width), F32)],
-        out_shape=[jax.ShapeDtypeStruct((rows, width), F32), jax.ShapeDtypeStruct((rows, width), BF16)],
-        compiler_params=params(20),
+        out_specs=pl.BlockSpec((rows, width), lambda i: (0, 0)),
+        scratch_shapes=[pltpu.VMEM((rows, width), F32)],
+        out_shape=jax.ShapeDtypeStruct((rows, width), dtype),
+        compiler_params=params(12),
         name="forward",
-    )(pltpu.with_memory_space_constraint(dense, pltpu.HBM), panels)
+    )(pltpu.with_memory_space_constraint(dense, pltpu.HBM), pltpu.with_memory_space_constraint(panels, pltpu.HBM), before)
 
 
 def one_hot(slot, slots):
@@ -218,24 +216,26 @@
     )(own, got, slot)
 
 
-def pack_columns_kernel(samples_ref, slot_ref, _, packed_ref):
+def pack_columns_kernel(samples_ref, slot_ref, _, packed_ref, held_ref, sem):
+    copy = pltpu.make_async_copy(samples_ref, held_ref, sem)
+    copy.start()
+    chosen = one_hot(slot_ref[...], packed_ref.shape[0])
+    copy.wait()
     packed_ref[...] = lax.dot_general(
-        one_hot(slot_ref[...], packed_ref.shape[0]),
-        samples_ref[...],
-        (((1,), (1,)), ((), ())),
-        preferred_element_type=F32,
+        chosen, held_ref[...], (((1,), (1,)), ((), ())), preferred_element_type=F32
     ).astype(BF16)
 
 
 def pack_columns(samples, slot, slots, before):
     return pl.pallas_call(
         pack_columns_kernel,
-        in_specs=[VMEM, VMEM, ANY],
+        in_specs=[HBM, VMEM, ANY],
         out_specs=VMEM,
         out_shape=jax.ShapeDtypeStruct((slots, samples.shape[0]), BF16),
+        scratch_shapes=[pltpu.VMEM(samples.shape, BF16), pltpu.SemaphoreType.DMA],
         compiler_params=params(8),
         name="pack_columns",
-    )(samples, slot, before)
+    )(pltpu.with_memory_space_constraint(samples, pltpu.HBM), slot, before)
 
 
 def owner_gram(received, count):
@@ -271,7 +271,8 @@
         )
     terms, dense = held
     columns = lax.psum_scatter(terms, "blk", scatter_dimension=0, tiled=False, axis_index_groups=halves)
-    own, partial = forward(dense, panels)
+    partial = forward(dense, panels, 1, BF16, slot)
+    own = forward(dense, panels, 0, F32, partial)
     got = lax.ppermute(partial, "blk", across)
     row_samples, row_packed = pack_rows(own, got, slot, slots)
     row_received = lax.all_to_all(row_packed.reshape(owners, capacity, width), "grp", 0, 0, tiled=True)

time: 151 us -> 151 us (level)
  Pallas kernels: 25.4 us -> 29.3 us
  local copies, waits for them, and re-layouts: 3.56 us -> 1.03 us
    ppermute x1, waiting for transfers between devices: 5.41 us -> 1.25 us  [body(): got = lax.ppermute(partial, 'blk', across)]
    pallas_call x1 -> x2, Pallas kernels: 5.84 us -> 8.75 us  [forward(): pl.pallas_call(forward_kernel, grid=(groups // 2,), in_specs=[pl.BlockSpe...]
    reduce_scatter x1, waiting for transfers between devices: 0.5 us -> 3.35 us  [body(): lax.psum_scatter(terms, 'blk', scatter_dimension=0, tiled=False, axis_ind...]
    unnamed x11 -> x7, local copies, waits for them, and re-layouts: 3.39 us -> 0.85 us
  transfers between devices with their start and end apart: 8 -> 8, of which waited for: 6 -> 6; matrix products, arithmetic and copies ran while one was open for 2% -> 2% of each run, Pallas kernels for 16% -> 18%
where the time goes in v4:
time: 151 us; the launch traced here: 150 us
  waiting for transfers between devices  43.6 us (29%)
  blocking collectives  29.9 us (20%)
  Pallas kernels  29.3 us (19%)
  starting transfers between devices  28.4 us (19%)
  between operations  14.2 us (9%)
  matrix products  2.09 us (1%)
  other arithmetic  1.53 us (1%)
    all_to_all x1, blocking collectives, body(): lax.all_to_all(row_packed.reshape(owners, capacity, width), 'grp', 0, 0,...  29.9 us
    ppermute x4, waiting for transfers between devices, body(): received = [lax.ppermute(part, 'blk', across) for part in leaving]  21.8 us
    all_to_all x1, waiting for transfers between devices, body(): lax.all_to_all(column_packed.reshape(owners, capacity, width), 'grp', 0,...  16.6 us
    pallas_call x4, Pallas kernels, strips(): pl.pallas_call(functools.partial(strip_kernel, start), grid_spec=pltpu.Pr...  14.8 us
    ppermute x4, starting transfers between devices, body(): received = [lax.ppermute(part, 'blk', across) for part in leaving]  14.7 us
    pallas_call x2, Pallas kernels, forward(): pl.pallas_call(forward_kernel, grid=(groups // 2,), in_specs=[pl.BlockSpe...  8.75 us
    all_to_all x1, starting transfers between devices, body(): lax.all_to_all(column_packed.reshape(owners, capacity, width), 'grp', 0,...  8.68 us
    ppermute x1, starting transfers between devices, body(): got = lax.ppermute(partial, 'blk', across)  4.93 us
  transfers between devices with their start and end apart: 8, of which 6 were waited for; matrix products, arithmetic and copies ran while one was open for 2% of the time, Pallas kernels for 18%

profile of v4, /device:TPU:24, one launch (start us, length us, event | category | flops | bytes accessed | tf_op | source)
XLA Modules:
  0.0 150.0 jit_solution(573219516226206247)
XLA Ops:
  7.2 0.7 all-gather.2.cloned.1.call-update
  7.9 0.0 reduce-scatter.2.cloned.1.call-start
  8.0 0.9 multiply_add_fusion
  8.8 0.1 copy.18
  8.9 0.1 reshape.40.mine_ref
  9.0 2.5 %prepare.1 = (bf16[9,128,128]{2,1,0:T(8,128)(2,1)S(1)}, bf16[27,128,128]{2,1,0:T(8,128)(2,1)}, bf16[18,128,128]{2,1,0:T(8,128)(2,1)}, bf16[6,128,128]{2,1,0:T(8,128)(2,1)}, bf16[6,128,128]{2,1,0:T(8,128)(2,1)}) custom-call(s32[1]{0:T(128)} %bitcast.1.first_ref, bf16[16,6,128,128]{3,2,1,0:T(8,128)(2,1)} %bitcast.39, bf16[512,256]{1,0:T(8,128)(2,1)} %q_ref.1, ...), custom_call_target="tpu_custom_call" | custom-call | tf_op jit(solution)/shard_map/prepare/pallas_call | solution.py:57
  11.5 4.9 %collective-permute-start = (bf16[27,128,128]{2,1,0:T(8,128)(2,1)}, bf16[27,128,128]{2,1,0:T(8,128)(2,1)}, u32[]{:S(2)}, u32[]{:S(2)}) collective-permute-start(bf16[27,128,128]{2,1,0:T(8,128)(2,1)} %get-tuple-element.19), channel_id=1, source_target_pairs={{0,256},{32,288},{64,320},{96,352},{128,384},{160,416},{192,448},{... | collective-permute-start | bytes 2654216 | tf_op jit(solution)/shard_map/ppermute | solution.py:263
  16.4 2.4 %collective-permute-start.3 = (bf16[18,128,128]{2,1,0:T(8,128)(2,1)}, bf16[18,128,128]{2,1,0:T(8,128)(2,1)}, u32[]{:S(2)}, u32[]{:S(2)}) collective-permute-start(bf16[18,128,128]{2,1,0:T(8,128)(2,1)} %get-tuple-element.23), channel_id=1, source_target_pairs={{0,256},{32,288},{64,320},{96,352},{128,384},{160,416},{192,448},{... | collective-permute-start | bytes 1769480 | tf_op jit(solution)/shard_map/ppermute | solution.py:263
  18.9 4.9 %collective-permute-start.1 = (bf16[6,128,128]{2,1,0:T(8,128)(2,1)}, bf16[6,128,128]{2,1,0:T(8,128)(2,1)}, u32[]{:S(2)}, u32[]{:S(2)}) collective-permute-start(bf16[6,128,128]{2,1,0:T(8,128)(2,1)} %get-tuple-element.21), channel_id=1, source_target_pairs={{0,256},{32,288},{64,320},{96,352},{128,384},{160,416},{192,448},{... | collective-permute-start | bytes 589832 | tf_op jit(solution)/shard_map/ppermute | solution.py:263
  23.8 2.4 %collective-permute-start.2 = (bf16[6,128,128]{2,1,0:T(8,128)(2,1)}, bf16[6,128,128]{2,1,0:T(8,128)(2,1)}, u32[]{:S(2)}, u32[]{:S(2)}) collective-permute-start(bf16[6,128,128]{2,1,0:T(8,128)(2,1)} %get-tuple-element.22), channel_id=1, source_target_pairs={{0,256},{32,288},{64,320},{96,352},{128,384},{160,416},{192,448},{... | collective-permute-start | bytes 589832 | tf_op jit(solution)/shard_map/ppermute | solution.py:263
  26.2 11.5 %collective-permute-done.qp_ref.b_ref = bf16[27,128,128]{2,1,0:T(8,128)(2,1)} collective-permute-done((bf16[27,128,128]{2,1,0:T(8,128)(2,1)}, bf16[27,128,128]{2,1,0:T(8,128)(2,1)}, u32[]{:S(2)}, u32[]{:S(2)}) %collective-permute-start) | collective-permute-done | bytes 884768 | tf_op jit(solution)/shard_map/ppermute | solution.py:263
  37.8 0.7 fusion.4.theirs_ref._
  38.4 4.5 %strips.4 = (bf16[8,256,512]{2,1,0:T(8,128)(2,1)}, bf16[8,1024,512]{2,1,0:T(8,128)(2,1)}) custom-call(s32[1]{0:T(128)} %bitcast.first_ref, s32[96]{0:T(128)S(1)} %reshape.40.mine_ref, s32[96]{0:T(128)S(1)} %fusion.4.theirs_ref._, bf16[9,128,128]{2,1,0:T(8,128)(2,1)S(1)} %get-tuple-element.20.q_ref, bf16[27,128,128]{2,1,0:T(8,128)(2,1)} %collective-permute-done.qp_ref.b_ref, ...), custom_call_target="tpu_custom_call" | custom-call | tf_op jit(solution)/shard_map/strips/pallas_call | solution.py:135
  43.0 7.4 %collective-permute-done.3.b_ref = bf16[18,128,128]{2,1,0:T(8,128)(2,1)} collective-permute-done((bf16[18,128,128]{2,1,0:T(8,128)(2,1)}, bf16[18,128,128]{2,1,0:T(8,128)(2,1)}, u32[]{:S(2)}, u32[]{:S(2)}) %collective-permute-start.3) | collective-permute-done | bytes 589856 | tf_op jit(solution)/shard_map/ppermute | solution.py:263
  50.4 4.4 %strips.5 = (bf16[8,256,512]{2,1,0:T(8,128)(2,1)}, bf16[8,1024,512]{2,1,0:T(8,128)(2,1)}) custom-call(s32[1]{0:T(128)} %bitcast.first_ref, s32[96]{0:T(128)S(1)} %reshape.40.mine_ref, s32[96]{0:T(128)S(1)} %fusion.4.theirs_ref._, bf16[9,128,128]{2,1,0:T(8,128)(2,1)S(1)} %get-tuple-element.20.q_ref, ...), custom_call_target="tpu_custom_call", output_to_operand_aliasing={{0}: (7, {}), {1}: (8, {})} | custom-call | tf_op jit(solution)/shard_map/strips/pallas_call | solution.py:135
  54.8 2.8 %collective-permute-done.2.b_ref = bf16[6,128,128]{2,1,0:T(8,128)(2,1)} collective-permute-done((bf16[6,128,128]{2,1,0:T(8,128)(2,1)}, bf16[6,128,128]{2,1,0:T(8,128)(2,1)}, u32[]{:S(2)}, u32[]{:S(2)}) %collective-permute-start.2) | collective-permute-done | bytes 196640 | tf_op jit(solution)/shard_map/ppermute | solution.py:263
  57.7 2.9 %strips.6 = (bf16[8,256,512]{2,1,0:T(8,128)(2,1)}, bf16[8,1024,512]{2,1,0:T(8,128)(2,1)}) custom-call(s32[1]{0:T(128)} %bitcast.first_ref, s32[96]{0:T(128)S(1)} %reshape.40.mine_ref, s32[96]{0:T(128)S(1)} %fusion.4.theirs_ref._, bf16[9,128,128]{2,1,0:T(8,128)(2,1)S(1)} %get-tuple-element.20.q_ref, ...), custom_call_target="tpu_custom_call", output_to_operand_aliasing={{0}: (7, {}), {1}: (8, {})} | custom-call | tf_op jit(solution)/shard_map/strips/pallas_call | solution.py:135
  60.6 2.9 %strips.7 = (bf16[8,256,512]{2,1,0:T(8,128)(2,1)}, bf16[8,1024,512]{2,1,0:T(8,128)(2,1)}) custom-call(s32[1]{0:T(128)} %bitcast.first_ref, s32[96]{0:T(128)S(1)} %reshape.40.mine_ref, s32[96]{0:T(128)S(1)} %fusion.4.theirs_ref._, bf16[9,128,128]{2,1,0:T(8,128)(2,1)S(1)} %get-tuple-element.20.q_ref, ...), custom_call_target="tpu_custom_call", output_to_operand_aliasing={{0}: (7, {}), {1}: (8, {})} | custom-call | tf_op jit(solution)/shard_map/strips/pallas_call | solution.py:135
  63.6 0.2 slots.1._.slot_ref
  63.8 4.4 %forward.2._ = bf16[512,256]{1,0:T(8,128)(2,1)S(1)} custom-call(bf16[8,1024,512]{2,1,0:T(8,128)(2,1)} %get-tuple-element.30.d_ref, bf16[8,512,256]{2,1,0:T(8,128)(2,1)} %bitcast.46, s32[1,512]{1,0:T(1,128)S(1)} %slots.1._.slot_ref), custom_call_target="tpu_custom_call" | custom-call | tf_op jit(solution)/shard_map/forward/pallas_call | solution.py:181
  68.2 4.9 %collective-permute-start.4 = (bf16[512,256]{1,0:T(8,128)(2,1)S(1)}, bf16[512,256]{1,0:T(8,128)(2,1)S(1)}, u32[]{:S(2)}, u32[]{:S(2)}) collective-permute-start(bf16[512,256]{1,0:T(8,128)(2,1)S(1)} %forward.2._), channel_id=1, source_target_pairs={{0,256},{32,288},{64,320},{96,352},{128,384},{160,416},{192,448},{... | collective-permute-start | bytes 786440 | tf_op jit(solution)/shard_map/ppermute | solution.py:276
  73.1 4.4 %forward.3.own_ref = f32[512,256]{1,0:T(8,128)S(1)} custom-call(bf16[8,1024,512]{2,1,0:T(8,128)(2,1)} %get-tuple-element.30.d_ref, bf16[8,512,256]{2,1,0:T(8,128)(2,1)} %bitcast.47, bf16[512,256]{1,0:T(8,128)(2,1)S(1)} %forward.2._), custom_call_target="tpu_custom_call" | custom-call | tf_op jit(solution)/shard_map/forward/pallas_call | solution.py:181
  77.5 1.2 collective-permute-done.4.got_ref
  78.7 0.8 pack_rows.1
  79.5 29.9 %all_to_all.10._ = bf16[32,32,256]{2,1,0:T(8,128)(2,1)S(1)} all-to-all(bf16[32,32,256]{2,1,0:T(8,128)(2,1)S(1)} %bitcast.44), channel_id=1, replica_groups=mesh['blk'=16,'grp'=32] {'grp'}, dimensions={0} | all-to-all | bytes 1048576 | tf_op jit(solution)/shard_map/all_to_all | solution.py:278
  109.4 3.3 %reduce-scatter.2.cloned.1.call-done = bf16[1,256,512]{2,1,0:T(8,128)(2,1)} async-done(((bf16[8,256,512]{2,1,0:T(8,128)(2,1)}), bf16[1,256,512]{2,1,0:T(8,128)(2,1)}) %reduce-scatter.2.cloned.1.call-update) | async-done | bytes 262160 | tf_op jit(solution)/shard_map/reduce_scatter | solution.py:273
  112.7 2.3 %pack_columns.1 = bf16[1024,256]{1,0:T(8,128)(2,1)} custom-call(bf16[256,512]{1,0:T(8,128)(2,1)} %bitcast.48, s32[1,512]{1,0:T(1,128)S(1)} %slots.1._.slot_ref, bf16[32,32,256]{2,1,0:T(8,128)(2,1)S(1)} %all_to_all.10._), custom_call_target="tpu_custom_call" | custom-call | tf_op jit(solution)/shard_map/pack_columns/pallas_call | solution.py:230
  115.0 8.7 %all-to-all-start.1 = ((bf16[32,32,256]{2,1,0:T(8,128)(2,1)}), bf16[32,32,256]{2,1,0:T(8,128)(2,1)S(1)}, u32[]{:S(2)}, u32[]{:S(2)}) async-start(bf16[32,32,256]{2,1,0:T(8,128)(2,1)} %bitcast.13), calls=%async_computation.2 | async-start | bytes 1048576 | tf_op jit(solution)/shard_map/all_to_all | solution.py:280
  123.7 1.0 fusion.2
  124.8 0.8 copy.19
  125.6 16.6 %all-to-all-done.1 = bf16[32,32,256]{2,1,0:T(8,128)(2,1)S(1)} async-done(((bf16[32,32,256]{2,1,0:T(8,128)(2,1)}), bf16[32,32,256]{2,1,0:T(8,128)(2,1)S(1)}, u32[]{:S(2)}, u32[]{:S(2)}) %all-to-all-start.1) | async-done | bytes 524320 | tf_op jit(solution)/shard_map/all_to_all | solution.py:280
  142.2 1.0 fusion.3
  (12 shorter events, 0.1 us)
Async XLA Ops:
  7.2 31.3 %copy-start = (bf16[1,1,16,6,128,128]{5,4,3,2,1,0:T(8,128)(2,1)S(1)}, bf16[1,1,16,6,128,128]{5,4,3,2,1,0:T(8,128)(2,1)}, u32[]{:S(2)}) copy-start(bf16[1,1,16,6,128,128]{5,4,3,2,1,0:T(8,128)(2,1)} %param.6) | copy-start | bytes 9437188
  7.2 56.6 %all-gather.2.cloned.1.call-start = ((), (), s32[]{:S(2)}) async-start(), calls=%async_computation.3 | async-start | bytes 2359296 | tf_op jit(solution)/shard_map/all_gather | solution.py:262
  7.9 104.8 %reduce-scatter.2.cloned.1.call-start = ((), (), s32[]{:S(2)}) async-start(), calls=%async_computation.4 | async-start | bytes 2359296 | tf_op jit(solution)/shard_map/reduce_scatter | solution.py:273
  11.5 26.2 %collective-permute-start = (bf16[27,128,128]{2,1,0:T(8,128)(2,1)}, bf16[27,128,128]{2,1,0:T(8,128)(2,1)}, u32[]{:S(2)}, u32[]{:S(2)}) collective-permute-start(bf16[27,128,128]{2,1,0:T(8,128)(2,1)} %get-tuple-element.19), channel_id=1, source_target_pairs={{0,256},{32,288},{64,320},{96,352},{128,384},{160,416},{192,448},{... | collective-permute-start | bytes 2654216 | tf_op jit(solution)/shard_map/ppermute | solution.py:263
  16.4 33.9 %collective-permute-start.3 = (bf16[18,128,128]{2,1,0:T(8,128)(2,1)}, bf16[18,128,128]{2,1,0:T(8,128)(2,1)}, u32[]{:S(2)}, u32[]{:S(2)}) collective-permute-start(bf16[18,128,128]{2,1,0:T(8,128)(2,1)} %get-tuple-element.23), channel_id=1, source_target_pairs={{0,256},{32,288},{64,320},{96,352},{128,384},{160,416},{192,448},{... | collective-permute-start | bytes 1769480 | tf_op jit(solution)/shard_map/ppermute | solution.py:263
  18.9 41.7 %collective-permute-start.1 = (bf16[6,128,128]{2,1,0:T(8,128)(2,1)}, bf16[6,128,128]{2,1,0:T(8,128)(2,1)}, u32[]{:S(2)}, u32[]{:S(2)}) collective-permute-start(bf16[6,128,128]{2,1,0:T(8,128)(2,1)} %get-tuple-element.21), channel_id=1, source_target_pairs={{0,256},{32,288},{64,320},{96,352},{128,384},{160,416},{192,448},{... | collective-permute-start | bytes 589832 | tf_op jit(solution)/shard_map/ppermute | solution.py:263
  23.8 33.9 %collective-permute-start.2 = (bf16[6,128,128]{2,1,0:T(8,128)(2,1)}, bf16[6,128,128]{2,1,0:T(8,128)(2,1)}, u32[]{:S(2)}, u32[]{:S(2)}) collective-permute-start(bf16[6,128,128]{2,1,0:T(8,128)(2,1)} %get-tuple-element.22), channel_id=1, source_target_pairs={{0,256},{32,288},{64,320},{96,352},{128,384},{160,416},{192,448},{... | collective-permute-start | bytes 589832 | tf_op jit(solution)/shard_map/ppermute | solution.py:263
  60.6 3.0 %copy-start.1 = (s32[512,1]{0,1:T(1,128)S(1)}, s32[512,1]{0,1:T(1,128)}, u32[]{:S(2)}) copy-start(s32[512,1]{0,1:T(1,128)} %param.11) | copy-start | bytes 6148
  68.2 10.6 %collective-permute-start.4 = (bf16[512,256]{1,0:T(8,128)(2,1)S(1)}, bf16[512,256]{1,0:T(8,128)(2,1)S(1)}, u32[]{:S(2)}, u32[]{:S(2)}) collective-permute-start(bf16[512,256]{1,0:T(8,128)(2,1)S(1)} %forward.2._), channel_id=1, source_target_pairs={{0,256},{32,288},{64,320},{96,352},{128,384},{160,416},{192,448},{... | collective-permute-start | bytes 786440 | tf_op jit(solution)/shard_map/ppermute | solution.py:276
  112.7 12.0 %copy-start.2 = (bf16[1,256,512]{2,1,0:T(8,128)(2,1)S(1)}, bf16[1,256,512]{2,1,0:T(8,128)(2,1)}, u32[]{:S(2)}) copy-start(bf16[1,256,512]{2,1,0:T(8,128)(2,1)} %reduce-scatter.2.cloned.1.call-done) | copy-start | bytes 786436
  115.0 27.1 %all-to-all-start.1 = ((bf16[32,32,256]{2,1,0:T(8,128)(2,1)}), bf16[32,32,256]{2,1,0:T(8,128)(2,1)S(1)}, u32[]{:S(2)}, u32[]{:S(2)}) async-start(bf16[32,32,256]{2,1,0:T(8,128)(2,1)} %bitcast.13), calls=%async_computation.2 | async-start | bytes 1048576 | tf_op jit(solution)/shard_map/all_to_all | solution.py:280
Sparse Core Ops, SparseCore 0:
  10.1 47.4 all-gather.1
  63.7 49.0 reduce-scatter.1

commit v5 on v4

--- a/solution.py
+++ b/solution.py
@@ -9,7 +9,7 @@
 
 F32 = jnp.float32
 BF16 = jnp.bfloat16
-PARTS = (3, 3, 1, 1)
+PARTS = (3, 3, 2)
 
 
 def params(mib):
@@ -98,65 +98,88 @@
     )(owner, before)
 
 
-def strip_kernel(start, first_ref, mine_ref, theirs_ref, q_ref, qp_ref, a_ref, b_ref, *refs):
-    c_ref, d_ref = refs[-2:]
-    k = a_ref.shape[1]
-    side = a_ref.shape[2]
-    rows = d_ref.shape[1] // 2
-    per = rows // side
-    head = 0 if start else q_ref.shape[0]
+def fill(d_ref, codes, source, block):
+    k, side, at_first = block
+    per = d_ref.shape[1] // side
     d_ref[...] = jnp.zeros(d_ref.shape, d_ref.dtype)
-    source = first_ref[0] + start + pl.program_id(0)
-    for base, codes in ((0, mine_ref), (rows, theirs_ref)):
-        for n in range(k):
-            code = codes[source * k + n]
-            at_row = pl.multiple_of(base + (code // per) * side, side)
-            at_col = pl.multiple_of((code % per) * side, side)
-            place = (0, pl.ds(at_row, side), pl.ds(at_col, side))
-            block = a_ref[0, n] if base == 0 else b_ref[head + pl.program_id(0) * k + n]
-            d_ref[place] = (d_ref[place].astype(F32) + block.astype(F32)).astype(d_ref.dtype)
-
-    def turned(ref):
-        down = c_ref.shape[1] // side
-        return jnp.concatenate(
-            [jnp.concatenate([ref[i * per + j] for j in range(per)], axis=1) for i in range(down)], axis=0
+    for n in range(k):
+        code = codes[source * k + n]
+        place = (
+            0,
+            pl.ds(pl.multiple_of((code // per) * side, side), side),
+            pl.ds(pl.multiple_of((code % per) * side, side), side),
         )
-
-    term = jnp.dot(turned(q_ref), d_ref[0, 0:rows, :], preferred_element_type=F32)
-    term += jnp.dot(turned(qp_ref), d_ref[0, rows:, :], preferred_element_type=F32)
-    c_ref[0] = term.astype(c_ref.dtype)
-
-
-def strips(start, size, first, mine, theirs, q, opening, blocks, received, shape, held):
+        d_ref[place] = (d_ref[place].astype(F32) + at_first(n).astype(F32)).astype(d_ref.dtype)
+
+
+def turned_dot(q_ref, d_ref, width):
+    side = q_ref.shape[1]
+    per = d_ref.shape[1] // side
+    q = jnp.concatenate(
+        [jnp.concatenate([q_ref[i * per + j] for j in range(per)], axis=1) for i in range(width // side)], axis=0
+    )
+    return jnp.dot(q, d_ref[0], preferred_element_type=F32)
+
+
+def own_kernel(first_ref, codes_ref, q_ref, a_ref, c_ref, d_ref):
+    fill(d_ref, codes_ref, first_ref[0] + pl.program_id(0), (a_ref.shape[1], a_ref.shape[2], lambda n: a_ref[0, n]))
+    c_ref[0] = turned_dot(q_ref, d_ref, c_ref.shape[1])
+
+
+def own_strips(first, codes, q, blocks, shape):
     _, k, side, _ = blocks.shape
     rows, width = shape
     groups = sum(PARTS)
-    whole = pl.BlockSpec(q.shape, lambda i, *_: (0, 0, 0))
+    return pl.pallas_call(
+        own_kernel,
+        grid_spec=pltpu.PrefetchScalarGridSpec(
+            num_scalar_prefetch=2,
+            grid=(groups,),
+            in_specs=[
+                pl.BlockSpec(q.shape, lambda i, *_: (0, 0, 0)),
+                pl.BlockSpec((1, k, side, side), lambda i, first, *_: (first[0] + i, 0, 0, 0)),
+            ],
+            out_specs=[
+                pl.BlockSpec((1, width, rows), lambda i, *_: (i, 0, 0)),
+                pl.BlockSpec((1, rows, rows), lambda i, *_: (i, 0, 0)),
+            ],
+        ),
+        out_shape=[pltpu.HBM((groups, width, rows), F32), pltpu.HBM((groups, rows, rows), BF16)],
+        compiler_params=params(10),
+        name="own_strips",
+    )(first, codes, q, blocks)
+
+
+def strip_kernel(start, first_ref, codes_ref, q_ref, b_ref, own_ref, *refs):
+    c_ref, d_ref = refs[-2:]
+    k = (b_ref.shape[0] - (0 if start else q_ref.shape[0])) // pl.num_programs(0)
+    skip = (0 if start else q_ref.shape[0]) + pl.program_id(0) * k
+    fill(d_ref, codes_ref, first_ref[0] + start + pl.program_id(0), (k, b_ref.shape[1], lambda n: b_ref[skip + n]))
+    c_ref[0] = (own_ref[0] + turned_dot(q_ref, d_ref, c_ref.shape[1])).astype(c_ref.dtype)
+
+
+def strips(start, size, first, codes, head, opening, received, own, held):
+    groups, width, rows = own.shape
+    side = opening.shape[1]
+    term = pl.BlockSpec((1, width, rows), lambda i, *_: (start + i, 0, 0))
     return pl.pallas_call(
         functools.partial(strip_kernel, start),
         grid_spec=pltpu.PrefetchScalarGridSpec(
-            num_scalar_prefetch=3,
+            num_scalar_prefetch=2,
             grid=(size,),
             in_specs=[
-                whole,
-                whole,
-                pl.BlockSpec((1, k, side, side), lambda i, first, *_: (first[0] + start + i, 0, 0, 0)),
+                pl.BlockSpec((head, side, side), lambda i, *_: (0, 0, 0)),
                 pl.BlockSpec(received.shape, lambda i, *_: (0, 0, 0)),
+                term,
             ]
             + [HBM] * len(held),
-            out_specs=[
-                pl.BlockSpec((1, width, rows), lambda i, *_: (start + i, 0, 0)),
-                pl.BlockSpec((1, 2 * rows, rows), lambda i, *_: (start + i, 0, 0)),
-            ],
+            out_specs=[term, pl.BlockSpec((1, rows, rows), lambda i, *_: (start + i, 0, 0))],
         ),
-        out_shape=[
-            pltpu.HBM((groups, width, rows), BF16),
-            pltpu.HBM((groups, 2 * rows, rows), BF16),
-        ],
-        input_output_aliases={7 + n: n for n in range(len(held))},
+        out_shape=[pltpu.HBM((groups, width, rows), BF16), pltpu.HBM((groups, rows, rows), BF16)],
+        input_output_aliases={5 + n: n for n in range(len(held))},
         compiler_params=params(10),
         name="strips",
-    )(first, mine, theirs, q, opening, blocks, received, *held)
+    )(first, codes, opening, received, pltpu.with_memory_space_constraint(own, pltpu.HBM), *held)
 
 
 def forward_kernel(d_ref, p_ref, _, out_ref, total_ref):
@@ -176,13 +199,13 @@
         out_ref[...] = total_ref[...].astype(out_ref.dtype)
 
 
-def forward(dense, panels, half, dtype, before):
+def forward(dense, panels, dtype, before):
     groups, rows, width = panels.shape
     return pl.pallas_call(
         forward_kernel,
         grid=(groups // 2,),
         in_specs=[
-            pl.BlockSpec((2, rows, rows), lambda i: (i, half, 0)),
+            pl.BlockSpec((2, rows, rows), lambda i: (i, 0, 0)),
             pl.BlockSpec((2, rows, width), lambda i: (i, 0, 0)),
             ANY,
         ],
@@ -264,15 +287,16 @@
     partner_codes = received[0][q.shape[0] - 1, 0, 0 : codes.shape[0]].astype(jnp.int32)
     slot = slots_of(row_owner.reshape(1, n_rows), owners, capacity, partner_codes)
 
+    own_terms, own_dense = own_strips(kept, codes, q, blocks, (n_rows, width))
     held = ()
     for j, size in enumerate(PARTS):
         held = strips(
-            sum(PARTS[:j]), size, kept, codes, partner_codes, q, received[0], blocks, received[j], (n_rows, width), held
+            sum(PARTS[:j]), size, kept, partner_codes, q.shape[0], received[0], received[j], own_terms, held
         )
     terms, dense = held
     columns = lax.psum_scatter(terms, "blk", scatter_dimension=0, tiled=False, axis_index_groups=halves)
-    partial = forward(dense, panels, 1, BF16, slot)
-    own = forward(dense, panels, 0, F32, partial)
+    partial = forward(dense, panels, BF16, slot)
+    own = forward(own_dense, panels, F32, partial)
     got = lax.ppermute(partial, "blk", across)
     row_samples, row_packed = pack_rows(own, got, slot, slots)
     row_received = lax.all_to_all(row_packed.reshape(owners, capacity, width), "grp", 0, 0, tiled=True)

time: 151 us -> 148 us (0.980)
  waiting for transfers between devices: 43.6 us -> 38.9 us
  Pallas kernels: 29.3 us -> 32.4 us
  starting transfers between devices: 28.4 us -> 25.9 us
  local copies, waits for them, and re-layouts: 1.03 us -> 2.91 us
    pallas_call x0 -> x1, Pallas kernels: none -> 5.88 us  [own_strips(): pl.pallas_call(own_kernel, grid_spec=pltpu.PrefetchScalarGridSpec(num_sca...]
    ppermute x4 -> x3, waiting for transfers between devices: 21.8 us -> 17 us  [body(): received = [lax.ppermute(part, 'blk', across) for part in leaving]]
    pallas_call x4 -> x3, Pallas kernels: 14.8 us -> 12.1 us  [strips(): pl.pallas_call(functools.partial(strip_kernel, start), grid_spec=pltpu.Pr...]
    ppermute x4 -> x3, starting transfers between devices: 14.7 us -> 12.3 us  [body(): received = [lax.ppermute(part, 'blk', across) for part in leaving]]
    unnamed x7, local copies, waits for them, and re-layouts: 0.85 us -> 2.73 us
  transfers between devices with their start and end apart: 8 -> 7, of which waited for: 6 -> 6; matrix products, arithmetic and copies ran while one was open for 2% -> 2% of each run, Pallas kernels for 18% -> 21%
where the time goes in v5:
time: 148 us; the launch traced here: 147 us
  waiting for transfers between devices  38.9 us (26%)
  Pallas kernels  32.4 us (22%)
  blocking collectives  29.9 us (20%)
  starting transfers between devices  25.9 us (18%)
  between operations  14.2 us (10%)
  local copies, waits for them, and re-layouts  2.91 us (2%)
  matrix products  2.09 us (1%)
    all_to_all x1, blocking collectives, body(): lax.all_to_all(row_packed.reshape(owners, capacity, width), 'grp', 0, 0,...  29.9 us
    ppermute x3, waiting for transfers between devices, body(): received = [lax.ppermute(part, 'blk', across) for part in leaving]  17 us
    all_to_all x1, waiting for transfers between devices, body(): lax.all_to_all(column_packed.reshape(owners, capacity, width), 'grp', 0,...  16.6 us
    ppermute x3, starting transfers between devices, body(): received = [lax.ppermute(part, 'blk', across) for part in leaving]  12.3 us
    pallas_call x3, Pallas kernels, strips(): pl.pallas_call(functools.partial(strip_kernel, start), grid_spec=pltpu.Pr...  12.1 us
    pallas_call x2, Pallas kernels, forward(): pl.pallas_call(forward_kernel, grid=(groups // 2,), in_specs=[pl.BlockSpe...  8.72 us
    all_to_all x1, starting transfers between devices, body(): lax.all_to_all(column_packed.reshape(owners, capacity, width), 'grp', 0,...  8.59 us
    pallas_call x1, Pallas kernels, own_strips(): pl.pallas_call(own_kernel, grid_spec=pltpu.PrefetchScalarGridSpec(num_sca...  5.88 us
  transfers between devices with their start and end apart: 7, of which 6 were waited for; matrix products, arithmetic and copies ran while one was open for 2% of the time, Pallas kernels for 21%

profile of v5, /device:TPU:24, one launch (start us, length us, event | category | flops | bytes accessed | tf_op | source)
XLA Modules:
  0.0 147.0 jit_solution(1560603237751763884)
XLA Ops:
  7.2 0.0 all-gather.2.cloned.1.call-start
  7.2 0.7 all-gather.2.cloned.1.call-update
  7.9 0.0 reduce-scatter.2.cloned.1.call-start
  8.0 0.7 multiply_add_fusion
  8.7 0.1 copy.16
  8.8 0.1 reshape.40.codes_ref
  8.9 2.5 %prepare.1 = (bf16[9,128,128]{2,1,0:T(8,128)(2,1)S(1)}, bf16[27,128,128]{2,1,0:T(8,128)(2,1)}, bf16[18,128,128]{2,1,0:T(8,128)(2,1)}, bf16[12,128,128]{2,1,0:T(8,128)(2,1)}) custom-call(s32[1]{0:T(128)} %bitcast.1.first_ref, bf16[16,6,128,128]{3,2,1,0:T(8,128)(2,1)} %bitcast.39, bf16[512,256]{1,0:T(8,128)(2,1)} %q_ref.1, f32[1,128]{1,0:T(1,128)S(1)} %pad_bitcast_fusion.code_ref), custom_call_target="tpu_custom_call" | custom-call | tf_op jit(solution)/shard_map/prepare/pallas_call | solution.py:57
  11.4 4.9 %collective-permute-start = (bf16[27,128,128]{2,1,0:T(8,128)(2,1)}, bf16[27,128,128]{2,1,0:T(8,128)(2,1)S(1)}, u32[]{:S(2)}, u32[]{:S(2)}) collective-permute-start(bf16[27,128,128]{2,1,0:T(8,128)(2,1)} %get-tuple-element.20), channel_id=1, source_target_pairs={{0,256},{32,288},{64,320},{96,352},{128,384},{160,416},{192,448},{... | collective-permute-start | bytes 2654216 | tf_op jit(solution)/shard_map/ppermute | solution.py:286
  16.3 2.4 %collective-permute-start.2 = (bf16[18,128,128]{2,1,0:T(8,128)(2,1)}, bf16[18,128,128]{2,1,0:T(8,128)(2,1)S(1)}, u32[]{:S(2)}, u32[]{:S(2)}) collective-permute-start(bf16[18,128,128]{2,1,0:T(8,128)(2,1)} %get-tuple-element.23), channel_id=1, source_target_pairs={{0,256},{32,288},{64,320},{96,352},{128,384},{160,416},{192,448},{... | collective-permute-start | bytes 1769480 | tf_op jit(solution)/shard_map/ppermute | solution.py:286
  18.7 4.9 %collective-permute-start.1 = (bf16[12,128,128]{2,1,0:T(8,128)(2,1)}, bf16[12,128,128]{2,1,0:T(8,128)(2,1)S(1)}, u32[]{:S(2)}, u32[]{:S(2)}) collective-permute-start(bf16[12,128,128]{2,1,0:T(8,128)(2,1)} %get-tuple-element.21), channel_id=1, source_target_pairs={{0,256},{32,288},{64,320},{96,352},{128,384},{160,416},{192,448},{... | collective-permute-start | bytes 1179656 | tf_op jit(solution)/shard_map/ppermute | solution.py:286
  23.7 1.9 %copy-done = bf16[1,1,16,6,128,128]{5,4,3,2,1,0:T(8,128)(2,1)S(1)} copy-done((bf16[1,1,16,6,128,128]{5,4,3,2,1,0:T(8,128)(2,1)S(1)}, bf16[1,1,16,6,128,128]{5,4,3,2,1,0:T(8,128)(2,1)}, u32[]{:S(2)}) %copy-start) | copy-done | bytes 3145752
  25.6 5.9 %own_strips.1 = (f32[8,256,512]{2,1,0:T(8,128)}, bf16[8,512,512]{2,1,0:T(8,128)(2,1)}) custom-call(s32[1]{0:T(128)} %bitcast.first_ref, s32[96]{0:T(128)S(1)} %reshape.40.codes_ref, bf16[9,128,128]{2,1,0:T(8,128)(2,1)S(1)} %get-tuple-element.18.q_ref, bf16[16,6,128,128]{3,2,1,0:T(8,128)(2,1)S(1)} %bitcast.40), custom_call_target="tpu_custom_call" | custom-call | tf_op jit(solution)/shard_map/own_strips/pallas_call | solution.py:133
  31.4 6.1 %collective-permute-done.q_ref.b_ref = bf16[27,128,128]{2,1,0:T(8,128)(2,1)S(1)} collective-permute-done((bf16[27,128,128]{2,1,0:T(8,128)(2,1)}, bf16[27,128,128]{2,1,0:T(8,128)(2,1)S(1)}, u32[]{:S(2)}, u32[]{:S(2)}) %collective-permute-start) | collective-permute-done | bytes 884768 | tf_op jit(solution)/shard_map/ppermute | solution.py:286
  37.5 4.5 %strips.3 = (bf16[8,256,512]{2,1,0:T(8,128)(2,1)}, bf16[8,512,512]{2,1,0:T(8,128)(2,1)}) custom-call(s32[1]{0:T(128)} %bitcast.first_ref, s32[96]{0:T(128)S(1)} %fusion.4.codes_ref._, bf16[27,128,128]{2,1,0:T(8,128)(2,1)S(1)} %collective-permute-done.q_ref.b_ref, bf16[27,128,128]{2,1,0:T(8,128)(2,1)S(1)} %collective-permute-done.q_ref.b_ref, ...), custom_call_target="tpu_custom_call" | custom-call | tf_op jit(solution)/shard_map/strips/pallas_call | solution.py:165
  42.0 8.1 %collective-permute-done.2.b_ref = bf16[18,128,128]{2,1,0:T(8,128)(2,1)S(1)} collective-permute-done((bf16[18,128,128]{2,1,0:T(8,128)(2,1)}, bf16[18,128,128]{2,1,0:T(8,128)(2,1)S(1)}, u32[]{:S(2)}, u32[]{:S(2)}) %collective-permute-start.2) | collective-permute-done | bytes 589856 | tf_op jit(solution)/shard_map/ppermute | solution.py:286
  50.1 4.5 %strips.4 = (bf16[8,256,512]{2,1,0:T(8,128)(2,1)}, bf16[8,512,512]{2,1,0:T(8,128)(2,1)}) custom-call(s32[1]{0:T(128)} %bitcast.first_ref, s32[96]{0:T(128)S(1)} %fusion.4.codes_ref._, bf16[27,128,128]{2,1,0:T(8,128)(2,1)S(1)} %collective-permute-done.q_ref.b_ref, ...), custom_call_target="tpu_custom_call", output_to_operand_aliasing={{0}: (5, {}), {1}: (6, {})} | custom-call | tf_op jit(solution)/shard_map/strips/pallas_call | solution.py:165
  54.6 2.8 %collective-permute-done.1.b_ref = bf16[12,128,128]{2,1,0:T(8,128)(2,1)S(1)} collective-permute-done((bf16[12,128,128]{2,1,0:T(8,128)(2,1)}, bf16[12,128,128]{2,1,0:T(8,128)(2,1)S(1)}, u32[]{:S(2)}, u32[]{:S(2)}) %collective-permute-start.1) | collective-permute-done | bytes 393248 | tf_op jit(solution)/shard_map/ppermute | solution.py:286
  57.4 3.1 %strips.5 = (bf16[8,256,512]{2,1,0:T(8,128)(2,1)}, bf16[8,512,512]{2,1,0:T(8,128)(2,1)}) custom-call(s32[1]{0:T(128)} %bitcast.first_ref, s32[96]{0:T(128)S(1)} %fusion.4.codes_ref._, bf16[27,128,128]{2,1,0:T(8,128)(2,1)S(1)} %collective-permute-done.q_ref.b_ref, ...), custom_call_target="tpu_custom_call", output_to_operand_aliasing={{0}: (5, {}), {1}: (6, {})} | custom-call | tf_op jit(solution)/shard_map/strips/pallas_call | solution.py:165
  60.6 0.2 slots.1._.slot_ref
  60.8 4.4 %forward.2._ = bf16[512,256]{1,0:T(8,128)(2,1)S(1)} custom-call(bf16[8,512,512]{2,1,0:T(8,128)(2,1)} %get-tuple-element.28.d_ref, bf16[8,512,256]{2,1,0:T(8,128)(2,1)} %bitcast.43, s32[1,512]{1,0:T(1,128)S(1)} %slots.1._.slot_ref), custom_call_target="tpu_custom_call" | custom-call | tf_op jit(solution)/shard_map/forward/pallas_call | solution.py:204
  65.2 4.9 %collective-permute-start.3 = (bf16[512,256]{1,0:T(8,128)(2,1)S(1)}, bf16[512,256]{1,0:T(8,128)(2,1)S(1)}, u32[]{:S(2)}, u32[]{:S(2)}) collective-permute-start(bf16[512,256]{1,0:T(8,128)(2,1)S(1)} %forward.2._), channel_id=1, source_target_pairs={{0,256},{32,288},{64,320},{96,352},{128,384},{160,416},{192,448},{... | collective-permute-start | bytes 786440 | tf_op jit(solution)/shard_map/ppermute | solution.py:300
  70.1 4.4 %forward.3.own_ref = f32[512,256]{1,0:T(8,128)S(1)} custom-call(bf16[8,512,512]{2,1,0:T(8,128)(2,1)} %get-tuple-element.19.d_ref, bf16[8,512,256]{2,1,0:T(8,128)(2,1)} %bitcast.44, bf16[512,256]{1,0:T(8,128)(2,1)S(1)} %forward.2._), custom_call_target="tpu_custom_call" | custom-call | tf_op jit(solution)/shard_map/forward/pallas_call | solution.py:204
  74.5 1.3 collective-permute-done.3.got_ref
  75.8 0.8 pack_rows.1
  76.5 29.9 %all_to_all.10._ = bf16[32,32,256]{2,1,0:T(8,128)(2,1)S(1)} all-to-all(bf16[32,32,256]{2,1,0:T(8,128)(2,1)S(1)} %bitcast.41), channel_id=1, replica_groups=mesh['blk'=16,'grp'=32] {'grp'}, dimensions={0} | all-to-all | bytes 1048576 | tf_op jit(solution)/shard_map/all_to_all | solution.py:302
  106.4 3.4 %reduce-scatter.2.cloned.1.call-done = bf16[1,256,512]{2,1,0:T(8,128)(2,1)} async-done(((bf16[8,256,512]{2,1,0:T(8,128)(2,1)}), bf16[1,256,512]{2,1,0:T(8,128)(2,1)}) %reduce-scatter.2.cloned.1.call-update) | async-done | bytes 262160 | tf_op jit(solution)/shard_map/reduce_scatter | solution.py:297
  109.8 2.3 %pack_columns.1 = bf16[1024,256]{1,0:T(8,128)(2,1)} custom-call(bf16[256,512]{1,0:T(8,128)(2,1)} %bitcast.45, s32[1,512]{1,0:T(1,128)S(1)} %slots.1._.slot_ref, bf16[32,32,256]{2,1,0:T(8,128)(2,1)S(1)} %all_to_all.10._), custom_call_target="tpu_custom_call" | custom-call | tf_op jit(solution)/shard_map/pack_columns/pallas_call | solution.py:253
  112.1 8.6 %all-to-all-start.1 = ((bf16[32,32,256]{2,1,0:T(8,128)(2,1)}), bf16[32,32,256]{2,1,0:T(8,128)(2,1)S(1)}, u32[]{:S(2)}, u32[]{:S(2)}) async-start(bf16[32,32,256]{2,1,0:T(8,128)(2,1)} %bitcast.13), calls=%async_computation.2 | async-start | bytes 1048576 | tf_op jit(solution)/shard_map/all_to_all | solution.py:304
  120.7 1.0 fusion.2
  121.7 0.8 copy.17
  122.6 16.6 %all-to-all-done.1 = bf16[32,32,256]{2,1,0:T(8,128)(2,1)S(1)} async-done(((bf16[32,32,256]{2,1,0:T(8,128)(2,1)}), bf16[32,32,256]{2,1,0:T(8,128)(2,1)S(1)}, u32[]{:S(2)}, u32[]{:S(2)}) %all-to-all-start.1) | async-done | bytes 524320 | tf_op jit(solution)/shard_map/all_to_all | solution.py:304
  139.1 1.0 fusion.3
  (10 shorter events, 0.1 us)
Async XLA Ops:
  7.2 53.7 %all-gather.2.cloned.1.call-start = ((), (), s32[]{:S(2)}) async-start(), calls=%async_computation.3 | async-start | bytes 2359296 | tf_op jit(solution)/shard_map/all_gather | solution.py:285
  7.9 101.9 %reduce-scatter.2.cloned.1.call-start = ((), (), s32[]{:S(2)}) async-start(), calls=%async_computation.4 | async-start | bytes 2359296 | tf_op jit(solution)/shard_map/reduce_scatter | solution.py:297
  11.4 26.1 %collective-permute-start = (bf16[27,128,128]{2,1,0:T(8,128)(2,1)}, bf16[27,128,128]{2,1,0:T(8,128)(2,1)S(1)}, u32[]{:S(2)}, u32[]{:S(2)}) collective-permute-start(bf16[27,128,128]{2,1,0:T(8,128)(2,1)} %get-tuple-element.20), channel_id=1, source_target_pairs={{0,256},{32,288},{64,320},{96,352},{128,384},{160,416},{192,448},{... | collective-permute-start | bytes 2654216 | tf_op jit(solution)/shard_map/ppermute | solution.py:286
  16.3 33.8 %collective-permute-start.2 = (bf16[18,128,128]{2,1,0:T(8,128)(2,1)}, bf16[18,128,128]{2,1,0:T(8,128)(2,1)S(1)}, u32[]{:S(2)}, u32[]{:S(2)}) collective-permute-start(bf16[18,128,128]{2,1,0:T(8,128)(2,1)} %get-tuple-element.23), channel_id=1, source_target_pairs={{0,256},{32,288},{64,320},{96,352},{128,384},{160,416},{192,448},{... | collective-permute-start | bytes 1769480 | tf_op jit(solution)/shard_map/ppermute | solution.py:286
  18.7 38.7 %collective-permute-start.1 = (bf16[12,128,128]{2,1,0:T(8,128)(2,1)}, bf16[12,128,128]{2,1,0:T(8,128)(2,1)S(1)}, u32[]{:S(2)}, u32[]{:S(2)}) collective-permute-start(bf16[12,128,128]{2,1,0:T(8,128)(2,1)} %get-tuple-element.21), channel_id=1, source_target_pairs={{0,256},{32,288},{64,320},{96,352},{128,384},{160,416},{192,448},{... | collective-permute-start | bytes 1179656 | tf_op jit(solution)/shard_map/ppermute | solution.py:286
  23.7 1.9 %copy-start = (bf16[1,1,16,6,128,128]{5,4,3,2,1,0:T(8,128)(2,1)S(1)}, bf16[1,1,16,6,128,128]{5,4,3,2,1,0:T(8,128)(2,1)}, u32[]{:S(2)}) copy-start(bf16[1,1,16,6,128,128]{5,4,3,2,1,0:T(8,128)(2,1)} %param.6) | copy-start | bytes 9437188
  57.4 3.2 %copy-start.1 = (s32[512,1]{0,1:T(1,128)S(1)}, s32[512,1]{0,1:T(1,128)}, u32[]{:S(2)}) copy-start(s32[512,1]{0,1:T(1,128)} %param.11) | copy-start | bytes 6148
  65.2 10.6 %collective-permute-start.3 = (bf16[512,256]{1,0:T(8,128)(2,1)S(1)}, bf16[512,256]{1,0:T(8,128)(2,1)S(1)}, u32[]{:S(2)}, u32[]{:S(2)}) collective-permute-start(bf16[512,256]{1,0:T(8,128)(2,1)S(1)} %forward.2._), channel_id=1, source_target_pairs={{0,256},{32,288},{64,320},{96,352},{128,384},{160,416},{192,448},{... | collective-permute-start | bytes 786440 | tf_op jit(solution)/shard_map/ppermute | solution.py:300
  109.8 12.0 %copy-start.2 = (bf16[1,256,512]{2,1,0:T(8,128)(2,1)S(1)}, bf16[1,256,512]{2,1,0:T(8,128)(2,1)}, u32[]{:S(2)}) copy-start(bf16[1,256,512]{2,1,0:T(8,128)(2,1)} %reduce-scatter.2.cloned.1.call-done) | copy-start | bytes 786436
  112.1 27.0 %all-to-all-start.1 = ((bf16[32,32,256]{2,1,0:T(8,128)(2,1)}), bf16[32,32,256]{2,1,0:T(8,128)(2,1)S(1)}, u32[]{:S(2)}, u32[]{:S(2)}) async-start(bf16[32,32,256]{2,1,0:T(8,128)(2,1)} %bitcast.13), calls=%async_computation.2 | async-start | bytes 1048576 | tf_op jit(solution)/shard_map/all_to_all | solution.py:304
Sparse Core Ops, SparseCore 0:
  10.1 47.4 all-gather.1
  60.7 49.0 reduce-scatter.1

commit v6 on v5

--- a/solution.py
+++ b/solution.py
@@ -9,7 +9,7 @@
 
 F32 = jnp.float32
 BF16 = jnp.bfloat16
-PARTS = (3, 3, 2)
+PARTS = (3, 3, 1, 1)
 
 
 def params(mib):

time: 148 us -> 147 us (level)
  waiting for transfers between devices: 38.9 us -> 33.8 us
  starting transfers between devices: 25.9 us -> 28.3 us
  Pallas kernels: 32.4 us -> 34.6 us
    ppermute x3 -> x4, waiting for transfers between devices: 17 us -> 11.9 us  [body(): received = [lax.ppermute(part, 'blk', across) for part in leaving]]
    ppermute x3 -> x4, starting transfers between devices: 12.3 us -> 14.7 us  [body(): received = [lax.ppermute(part, 'blk', across) for part in leaving]]
    pallas_call x3 -> x4, Pallas kernels: 12.1 us -> 14.3 us  [strips(): pl.pallas_call(functools.partial(strip_kernel, start), grid_spec=pltpu.Pr...]
  transfers between devices with their start and end apart: 7 -> 8, of which waited for: 6 -> 6; matrix products, arithmetic and copies ran while one was open for 2% -> 2% of each run, Pallas kernels for 21% -> 22%
where the time goes in v6:
time: 147 us
  Pallas kernels  34.6 us (24%)
  waiting for transfers between devices  33.8 us (23%)
  blocking collectives  29.9 us (20%)
  starting transfers between devices  28.3 us (19%)
  between operations  14.2 us (10%)
  local copies, waits for them, and re-layouts  2.91 us (2%)
  matrix products  2.09 us (1%)
    all_to_all x1, blocking collectives, body(): lax.all_to_all(row_packed.reshape(owners, capacity, width), 'grp', 0, 0,...  29.9 us
    all_to_all x1, waiting for transfers between devices, body(): lax.all_to_all(column_packed.reshape(owners, capacity, width), 'grp', 0,...  16.6 us
    ppermute x4, starting transfers between devices, body(): received = [lax.ppermute(part, 'blk', across) for part in leaving]  14.7 us
    pallas_call x4, Pallas kernels, strips(): pl.pallas_call(functools.partial(strip_kernel, start), grid_spec=pltpu.Pr...  14.3 us
    ppermute x4, waiting for transfers between devices, body(): received = [lax.ppermute(part, 'blk', across) for part in leaving]  11.9 us
    pallas_call x2, Pallas kernels, forward(): pl.pallas_call(forward_kernel, grid=(groups // 2,), in_specs=[pl.BlockSpe...  8.72 us
    all_to_all x1, starting transfers between devices, body(): lax.all_to_all(column_packed.reshape(owners, capacity, width), 'grp', 0,...  8.64 us
    pallas_call x1, Pallas kernels, own_strips(): pl.pallas_call(own_kernel, grid_spec=pltpu.PrefetchScalarGridSpec(num_sca...  5.86 us
  transfers between devices with their start and end apart: 8, of which 6 were waited for; matrix products, arithmetic and copies ran while one was open for 2% of the time, Pallas kernels for 22%

profile of v6, /device:TPU:24, one launch (start us, length us, event | category | flops | bytes accessed | tf_op | source)
XLA Modules:
  0.0 146.6 jit_solution(14481552937498613660)
XLA Ops:
  7.2 0.7 all-gather.2.cloned.1.call-update
  8.0 0.7 multiply_add_fusion
  8.7 0.1 copy.18
  8.8 0.1 reshape.40.codes_ref
  8.9 2.5 %prepare.1 = (bf16[9,128,128]{2,1,0:T(8,128)(2,1)S(1)}, bf16[27,128,128]{2,1,0:T(8,128)(2,1)}, bf16[18,128,128]{2,1,0:T(8,128)(2,1)}, bf16[6,128,128]{2,1,0:T(8,128)(2,1)}, bf16[6,128,128]{2,1,0:T(8,128)(2,1)}) custom-call(s32[1]{0:T(128)} %bitcast.1.first_ref, bf16[16,6,128,128]{3,2,1,0:T(8,128)(2,1)} %bitcast.39, bf16[512,256]{1,0:T(8,128)(2,1)} %q_ref.1, ...), custom_call_target="tpu_custom_call" | custom-call | tf_op jit(solution)/shard_map/prepare/pallas_call | solution.py:57
  11.3 4.9 %collective-permute-start = (bf16[27,128,128]{2,1,0:T(8,128)(2,1)}, bf16[27,128,128]{2,1,0:T(8,128)(2,1)S(1)}, u32[]{:S(2)}, u32[]{:S(2)}) collective-permute-start(bf16[27,128,128]{2,1,0:T(8,128)(2,1)} %get-tuple-element.23), channel_id=1, source_target_pairs={{0,256},{32,288},{64,320},{96,352},{128,384},{160,416},{192,448},{... | collective-permute-start | bytes 2654216 | tf_op jit(solution)/shard_map/ppermute | solution.py:286
  16.3 2.4 %collective-permute-start.3 = (bf16[18,128,128]{2,1,0:T(8,128)(2,1)}, bf16[18,128,128]{2,1,0:T(8,128)(2,1)S(1)}, u32[]{:S(2)}, u32[]{:S(2)}) collective-permute-start(bf16[18,128,128]{2,1,0:T(8,128)(2,1)} %get-tuple-element.27), channel_id=1, source_target_pairs={{0,256},{32,288},{64,320},{96,352},{128,384},{160,416},{192,448},{... | collective-permute-start | bytes 1769480 | tf_op jit(solution)/shard_map/ppermute | solution.py:286
  18.7 4.9 %collective-permute-start.2 = (bf16[6,128,128]{2,1,0:T(8,128)(2,1)}, bf16[6,128,128]{2,1,0:T(8,128)(2,1)S(1)}, u32[]{:S(2)}, u32[]{:S(2)}) collective-permute-start(bf16[6,128,128]{2,1,0:T(8,128)(2,1)} %get-tuple-element.26), channel_id=1, source_target_pairs={{0,256},{32,288},{64,320},{96,352},{128,384},{160,416},{192,448},{... | collective-permute-start | bytes 589832 | tf_op jit(solution)/shard_map/ppermute | solution.py:286
  23.6 2.4 %collective-permute-start.1 = (bf16[6,128,128]{2,1,0:T(8,128)(2,1)}, bf16[6,128,128]{2,1,0:T(8,128)(2,1)S(1)}, u32[]{:S(2)}, u32[]{:S(2)}) collective-permute-start(bf16[6,128,128]{2,1,0:T(8,128)(2,1)} %get-tuple-element.24), channel_id=1, source_target_pairs={{0,256},{32,288},{64,320},{96,352},{128,384},{160,416},{192,448},{... | collective-permute-start | bytes 589832 | tf_op jit(solution)/shard_map/ppermute | solution.py:286
  26.1 1.9 %copy-done = bf16[1,1,16,6,128,128]{5,4,3,2,1,0:T(8,128)(2,1)S(1)} copy-done((bf16[1,1,16,6,128,128]{5,4,3,2,1,0:T(8,128)(2,1)S(1)}, bf16[1,1,16,6,128,128]{5,4,3,2,1,0:T(8,128)(2,1)}, u32[]{:S(2)}) %copy-start) | copy-done | bytes 3145752
  28.0 5.9 %own_strips.1 = (f32[8,256,512]{2,1,0:T(8,128)}, bf16[8,512,512]{2,1,0:T(8,128)(2,1)}) custom-call(s32[1]{0:T(128)} %bitcast.first_ref, s32[96]{0:T(128)S(1)} %reshape.40.codes_ref, bf16[9,128,128]{2,1,0:T(8,128)(2,1)S(1)} %get-tuple-element.21.q_ref, bf16[16,6,128,128]{3,2,1,0:T(8,128)(2,1)S(1)} %bitcast.40), custom_call_target="tpu_custom_call" | custom-call | tf_op jit(solution)/shard_map/own_strips/pallas_call | solution.py:133
  33.8 3.7 %collective-permute-done.q_ref.b_ref = bf16[27,128,128]{2,1,0:T(8,128)(2,1)S(1)} collective-permute-done((bf16[27,128,128]{2,1,0:T(8,128)(2,1)}, bf16[27,128,128]{2,1,0:T(8,128)(2,1)S(1)}, u32[]{:S(2)}, u32[]{:S(2)}) %collective-permute-start) | collective-permute-done | bytes 884768 | tf_op jit(solution)/shard_map/ppermute | solution.py:286
  37.5 4.5 %strips.4 = (bf16[8,256,512]{2,1,0:T(8,128)(2,1)}, bf16[8,512,512]{2,1,0:T(8,128)(2,1)}) custom-call(s32[1]{0:T(128)} %bitcast.first_ref, s32[96]{0:T(128)S(1)} %fusion.4.codes_ref._, bf16[27,128,128]{2,1,0:T(8,128)(2,1)S(1)} %collective-permute-done.q_ref.b_ref, bf16[27,128,128]{2,1,0:T(8,128)(2,1)S(1)} %collective-permute-done.q_ref.b_ref, ...), custom_call_target="tpu_custom_call" | custom-call | tf_op jit(solution)/shard_map/strips/pallas_call | solution.py:165
  42.0 8.2 %collective-permute-done.3.b_ref = bf16[18,128,128]{2,1,0:T(8,128)(2,1)S(1)} collective-permute-done((bf16[18,128,128]{2,1,0:T(8,128)(2,1)}, bf16[18,128,128]{2,1,0:T(8,128)(2,1)S(1)}, u32[]{:S(2)}, u32[]{:S(2)}) %collective-permute-start.3) | collective-permute-done | bytes 589856 | tf_op jit(solution)/shard_map/ppermute | solution.py:286
  50.1 4.5 %strips.5 = (bf16[8,256,512]{2,1,0:T(8,128)(2,1)}, bf16[8,512,512]{2,1,0:T(8,128)(2,1)}) custom-call(s32[1]{0:T(128)} %bitcast.first_ref, s32[96]{0:T(128)S(1)} %fusion.4.codes_ref._, bf16[27,128,128]{2,1,0:T(8,128)(2,1)S(1)} %collective-permute-done.q_ref.b_ref, ...), custom_call_target="tpu_custom_call", output_to_operand_aliasing={{0}: (5, {}), {1}: (6, {})} | custom-call | tf_op jit(solution)/shard_map/strips/pallas_call | solution.py:165
  54.6 2.7 %strips.6 = (bf16[8,256,512]{2,1,0:T(8,128)(2,1)}, bf16[8,512,512]{2,1,0:T(8,128)(2,1)}) custom-call(s32[1]{0:T(128)} %bitcast.first_ref, s32[96]{0:T(128)S(1)} %fusion.4.codes_ref._, bf16[27,128,128]{2,1,0:T(8,128)(2,1)S(1)} %collective-permute-done.q_ref.b_ref, ...), custom_call_target="tpu_custom_call", output_to_operand_aliasing={{0}: (5, {}), {1}: (6, {})} | custom-call | tf_op jit(solution)/shard_map/strips/pallas_call | solution.py:165
  57.3 0.1 collective-permute-done.1.b_ref
  57.4 2.7 %strips.7 = (bf16[8,256,512]{2,1,0:T(8,128)(2,1)}, bf16[8,512,512]{2,1,0:T(8,128)(2,1)}) custom-call(s32[1]{0:T(128)} %bitcast.first_ref, s32[96]{0:T(128)S(1)} %fusion.4.codes_ref._, bf16[27,128,128]{2,1,0:T(8,128)(2,1)S(1)} %collective-permute-done.q_ref.b_ref, ...), custom_call_target="tpu_custom_call", output_to_operand_aliasing={{0}: (5, {}), {1}: (6, {})} | custom-call | tf_op jit(solution)/shard_map/strips/pallas_call | solution.py:165
  60.1 0.2 slots.1._.slot_ref
  60.4 4.4 %forward.2._ = bf16[512,256]{1,0:T(8,128)(2,1)S(1)} custom-call(bf16[8,512,512]{2,1,0:T(8,128)(2,1)} %get-tuple-element.34.d_ref, bf16[8,512,256]{2,1,0:T(8,128)(2,1)} %bitcast.43, s32[1,512]{1,0:T(1,128)S(1)} %slots.1._.slot_ref), custom_call_target="tpu_custom_call" | custom-call | tf_op jit(solution)/shard_map/forward/pallas_call | solution.py:204
  64.7 4.9 %collective-permute-start.4 = (bf16[512,256]{1,0:T(8,128)(2,1)S(1)}, bf16[512,256]{1,0:T(8,128)(2,1)S(1)}, u32[]{:S(2)}, u32[]{:S(2)}) collective-permute-start(bf16[512,256]{1,0:T(8,128)(2,1)S(1)} %forward.2._), channel_id=1, source_target_pairs={{0,256},{32,288},{64,320},{96,352},{128,384},{160,416},{192,448},{... | collective-permute-start | bytes 786440 | tf_op jit(solution)/shard_map/ppermute | solution.py:300
  69.7 4.4 %forward.3.own_ref = f32[512,256]{1,0:T(8,128)S(1)} custom-call(bf16[8,512,512]{2,1,0:T(8,128)(2,1)} %get-tuple-element.22.d_ref, bf16[8,512,256]{2,1,0:T(8,128)(2,1)} %bitcast.44, bf16[512,256]{1,0:T(8,128)(2,1)S(1)} %forward.2._), custom_call_target="tpu_custom_call" | custom-call | tf_op jit(solution)/shard_map/forward/pallas_call | solution.py:204
  74.0 1.3 collective-permute-done.4.got_ref
  75.3 0.8 pack_rows.1
  76.1 29.9 %all_to_all.10._ = bf16[32,32,256]{2,1,0:T(8,128)(2,1)S(1)} all-to-all(bf16[32,32,256]{2,1,0:T(8,128)(2,1)S(1)} %bitcast.41), channel_id=1, replica_groups=mesh['blk'=16,'grp'=32] {'grp'}, dimensions={0} | all-to-all | bytes 1048576 | tf_op jit(solution)/shard_map/all_to_all | solution.py:302
  105.9 3.4 %reduce-scatter.2.cloned.1.call-done = bf16[1,256,512]{2,1,0:T(8,128)(2,1)} async-done(((bf16[8,256,512]{2,1,0:T(8,128)(2,1)}), bf16[1,256,512]{2,1,0:T(8,128)(2,1)}) %reduce-scatter.2.cloned.1.call-update) | async-done | bytes 262160 | tf_op jit(solution)/shard_map/reduce_scatter | solution.py:297
  109.3 2.3 %pack_columns.1 = bf16[1024,256]{1,0:T(8,128)(2,1)} custom-call(bf16[256,512]{1,0:T(8,128)(2,1)} %bitcast.45, s32[1,512]{1,0:T(1,128)S(1)} %slots.1._.slot_ref, bf16[32,32,256]{2,1,0:T(8,128)(2,1)S(1)} %all_to_all.10._), custom_call_target="tpu_custom_call" | custom-call | tf_op jit(solution)/shard_map/pack_columns/pallas_call | solution.py:253
  111.6 8.6 %all-to-all-start.1 = ((bf16[32,32,256]{2,1,0:T(8,128)(2,1)}), bf16[32,32,256]{2,1,0:T(8,128)(2,1)S(1)}, u32[]{:S(2)}, u32[]{:S(2)}) async-start(bf16[32,32,256]{2,1,0:T(8,128)(2,1)} %bitcast.13), calls=%async_computation.2 | async-start | bytes 1048576 | tf_op jit(solution)/shard_map/all_to_all | solution.py:304
  120.2 1.0 fusion.2
  121.3 0.8 copy.19
  122.1 16.6 %all-to-all-done.1 = bf16[32,32,256]{2,1,0:T(8,128)(2,1)S(1)} async-done(((bf16[32,32,256]{2,1,0:T(8,128)(2,1)}), bf16[32,32,256]{2,1,0:T(8,128)(2,1)S(1)}, u32[]{:S(2)}, u32[]{:S(2)}) %all-to-all-start.1) | async-done | bytes 524320 | tf_op jit(solution)/shard_map/all_to_all | solution.py:304
  138.7 1.0 fusion.3
  (13 shorter events, 0.1 us)
Async XLA Ops:
  7.2 53.2 %all-gather.2.cloned.1.call-start = ((), (), s32[]{:S(2)}) async-start(), calls=%async_computation.3 | async-start | bytes 2359296 | tf_op jit(solution)/shard_map/all_gather | solution.py:285
  7.9 101.4 %reduce-scatter.2.cloned.1.call-start = ((), (), s32[]{:S(2)}) async-start(), calls=%async_computation.4 | async-start | bytes 2359296 | tf_op jit(solution)/shard_map/reduce_scatter | solution.py:297
  11.3 26.1 %collective-permute-start = (bf16[27,128,128]{2,1,0:T(8,128)(2,1)}, bf16[27,128,128]{2,1,0:T(8,128)(2,1)S(1)}, u32[]{:S(2)}, u32[]{:S(2)}) collective-permute-start(bf16[27,128,128]{2,1,0:T(8,128)(2,1)} %get-tuple-element.23), channel_id=1, source_target_pairs={{0,256},{32,288},{64,320},{96,352},{128,384},{160,416},{192,448},{... | collective-permute-start | bytes 2654216 | tf_op jit(solution)/shard_map/ppermute | solution.py:286
  16.3 33.8 %collective-permute-start.3 = (bf16[18,128,128]{2,1,0:T(8,128)(2,1)}, bf16[18,128,128]{2,1,0:T(8,128)(2,1)S(1)}, u32[]{:S(2)}, u32[]{:S(2)}) collective-permute-start(bf16[18,128,128]{2,1,0:T(8,128)(2,1)} %get-tuple-element.27), channel_id=1, source_target_pairs={{0,256},{32,288},{64,320},{96,352},{128,384},{160,416},{192,448},{... | collective-permute-start | bytes 1769480 | tf_op jit(solution)/shard_map/ppermute | solution.py:286
  18.7 35.9 %collective-permute-start.2 = (bf16[6,128,128]{2,1,0:T(8,128)(2,1)}, bf16[6,128,128]{2,1,0:T(8,128)(2,1)S(1)}, u32[]{:S(2)}, u32[]{:S(2)}) collective-permute-start(bf16[6,128,128]{2,1,0:T(8,128)(2,1)} %get-tuple-element.26), channel_id=1, source_target_pairs={{0,256},{32,288},{64,320},{96,352},{128,384},{160,416},{192,448},{... | collective-permute-start | bytes 589832 | tf_op jit(solution)/shard_map/ppermute | solution.py:286
  23.6 33.8 %collective-permute-start.1 = (bf16[6,128,128]{2,1,0:T(8,128)(2,1)}, bf16[6,128,128]{2,1,0:T(8,128)(2,1)S(1)}, u32[]{:S(2)}, u32[]{:S(2)}) collective-permute-start(bf16[6,128,128]{2,1,0:T(8,128)(2,1)} %get-tuple-element.24), channel_id=1, source_target_pairs={{0,256},{32,288},{64,320},{96,352},{128,384},{160,416},{192,448},{... | collective-permute-start | bytes 589832 | tf_op jit(solution)/shard_map/ppermute | solution.py:286
  26.1 1.9 %copy-start = (bf16[1,1,16,6,128,128]{5,4,3,2,1,0:T(8,128)(2,1)S(1)}, bf16[1,1,16,6,128,128]{5,4,3,2,1,0:T(8,128)(2,1)}, u32[]{:S(2)}) copy-start(bf16[1,1,16,6,128,128]{5,4,3,2,1,0:T(8,128)(2,1)} %param.6) | copy-start | bytes 9437188
  57.4 2.7 %copy-start.1 = (s32[512,1]{0,1:T(1,128)S(1)}, s32[512,1]{0,1:T(1,128)}, u32[]{:S(2)}) copy-start(s32[512,1]{0,1:T(1,128)} %param.11) | copy-start | bytes 6148
  64.7 10.6 %collective-permute-start.4 = (bf16[512,256]{1,0:T(8,128)(2,1)S(1)}, bf16[512,256]{1,0:T(8,128)(2,1)S(1)}, u32[]{:S(2)}, u32[]{:S(2)}) collective-permute-start(bf16[512,256]{1,0:T(8,128)(2,1)S(1)} %forward.2._), channel_id=1, source_target_pairs={{0,256},{32,288},{64,320},{96,352},{128,384},{160,416},{192,448},{... | collective-permute-start | bytes 786440 | tf_op jit(solution)/shard_map/ppermute | solution.py:300
  109.3 12.0 %copy-start.2 = (bf16[1,256,512]{2,1,0:T(8,128)(2,1)S(1)}, bf16[1,256,512]{2,1,0:T(8,128)(2,1)}, u32[]{:S(2)}) copy-start(bf16[1,256,512]{2,1,0:T(8,128)(2,1)} %reduce-scatter.2.cloned.1.call-done) | copy-start | bytes 786436
  111.6 27.1 %all-to-all-start.1 = ((bf16[32,32,256]{2,1,0:T(8,128)(2,1)}), bf16[32,32,256]{2,1,0:T(8,128)(2,1)S(1)}, u32[]{:S(2)}, u32[]{:S(2)}) async-start(bf16[32,32,256]{2,1,0:T(8,128)(2,1)} %bitcast.13), calls=%async_computation.2 | async-start | bytes 1048576 | tf_op jit(solution)/shard_map/all_to_all | solution.py:304
Sparse Core Ops, SparseCore 0:
  10.1 47.4 all-gather.1
  60.4 48.8 reduce-scatter.1
